TPU v7x, 32 devices: a whole 2x2x4 slice. The times are simulated.
32 devices in a mesh: grp: 2 (over core), row: 4 (over y, x), col: 4 (over z).
Axes of the slice: x: 2, y: 2, z: 4, core: 2. Of those that a mesh axis runs over, the one named last changes fastest.
Arguments:
- root_inverse: bfloat16 [12288, 12288], P(('grp', 'row'), 'col'), may hold values from -0.0546875 to 0.0546875
- child_inverse: bfloat16 [2, 8192, 8192], P('grp', 'row', 'col'), may hold values from -0.0625 to 0.0625
- coupling: bfloat16 [2, 1536, 8192], P('grp', 'col', 'row'), may hold values from -0.0625 to 0.0625
- child_weights: bfloat16 [2, 8192], P('grp', 'col'), may hold values from 0.5 to 2
- root_weights: bfloat16 [12288], P('col'), may hold values from 0.5 to 2
- parent_blocks: int32 [2, 12], replicated, may hold values from 0 to 95, as said below
Outputs:
- grad_root: bfloat16 [12288, 12288], P(('grp', 'row'), 'col')
- grad_child: bfloat16 [2, 8192, 8192], P('grp', 'row', 'col')
- grad_coupling: bfloat16 [2, 1536, 8192], P('grp', 'col', 'row')
Inputs may be any that keep to these rules, and one draw needn't show every extreme that they name: `parent_blocks`: within one child the 12 blocks are distinct; child 0 always names block 0 and block 12288 // 128 - 1; the two children may share blocks.
All inputs are finite; a program needn't handle non-finite values.
Results may differ from a plain program's by a relative error of at most 0.0059.
Values may be sent and summed in bfloat16 or wider, within the bound.
No kernel may reach another device: no remote copies, remote signals or barrier semaphores. Data moves between devices by JAX's collectives and lax.ppermute only.
A program may use at most 128 MiB of HBM per device.

v0:
```python
import jax
import jax.numpy as jnp
from jax import lax
from jax.sharding import PartitionSpec as P

BW = 128


def local(root_inverse, child_inverse, coupling, child_weights, root_weights, parent_blocks):
    col_index = lax.axis_index("col")
    col_count = lax.axis_size("col")
    root_rows, root_cols = root_inverse.shape
    local_blocks = root_cols // BW
    share_cols = coupling.shape[1]
    width = share_cols * col_count
    block_count = width // BW
    highest = lax.Precision.HIGHEST
    offset = parent_blocks - col_index * local_blocks
    block_ids = jnp.arange(local_blocks, dtype=jnp.int32)
    owners = [
        (offset[child][:, None] == block_ids[None, :]).astype(jnp.float32) for child in range(2)
    ]
    root_blocks = root_inverse.astype(jnp.float32).reshape(root_rows, local_blocks, BW)
    picks = []
    for child in range(2):
        taken = jnp.einsum("rkb,jk->rjb", root_blocks, owners[child], precision=highest)
        picks.append(taken.reshape(root_rows, width))
    picked = jnp.stack(picks, axis=1)
    selected = lax.psum(picked.astype(jnp.bfloat16), "col")
    mine = lax.dynamic_slice_in_dim(selected, col_index * share_cols, share_cols, 2)
    margin_part = jnp.concatenate(
        [
            jnp.dot(selected[:, child, :].T, mine[:, child, :], preferred_element_type=jnp.float32)
            for child in range(2)
        ],
        axis=0,
    )
    margin = lax.psum_scatter(margin_part, ("grp", "row"), scatter_dimension=0, tiled=True).astype(
        jnp.bfloat16
    )
    factor = child_inverse[0]
    links = coupling[0]
    weights = child_weights[0].astype(jnp.float32)
    links_all = lax.all_gather(links, "col", axis=0, tiled=True)
    solved = lax.psum_scatter(
        jnp.dot(links_all, factor, preferred_element_type=jnp.float32),
        "row",
        scatter_dimension=0,
        tiled=True,
    ).astype(jnp.bfloat16)
    solved_all = lax.all_gather(solved, "row", axis=0, tiled=True)
    scaled = (solved.astype(jnp.float32) * weights[None, :]).astype(jnp.bfloat16)
    adjoint_t = lax.psum_scatter(
        jnp.dot(solved_all, scaled.T, preferred_element_type=jnp.float32),
        "col",
        scatter_dimension=0,
        tiled=True,
    ).astype(jnp.bfloat16)
    adjoint_cols = lax.all_gather(adjoint_t, ("grp", "row"), axis=1, tiled=True).reshape(
        share_cols, 2, width
    )
    lifted = jnp.stack(
        [
            jnp.dot(
                selected[:, child, :],
                adjoint_cols[:, child, :].T,
                preferred_element_type=jnp.float32,
            )
            for child in range(2)
        ],
        axis=1,
    ).astype(jnp.bfloat16)
    lifted_all = lax.all_gather(lifted, "col", axis=2, tiled=True).reshape(
        root_rows, 2, block_count, BW
    )
    placed = jnp.zeros((root_rows, local_blocks, BW), jnp.float32)
    for child in range(2):
        spread = lifted_all[:, child].astype(jnp.float32)
        placed = placed + jnp.einsum("rjb,jk->rkb", spread, owners[child], precision=highest)
    placed = placed.reshape(root_rows, root_cols)
    root_scale = root_weights.astype(jnp.float32)[None, :]
    grad_root = (2.0 * root_inverse.astype(jnp.float32) * root_scale + 2.0 * placed).astype(
        jnp.bfloat16
    )
    margin_row = lax.all_gather(margin, "col", axis=1, tiled=True)
    pulled = (
        2.0 * jnp.dot(margin_row, solved_all, preferred_element_type=jnp.float32) * weights[None, :]
    ).astype(jnp.bfloat16)
    pulled_all = lax.all_gather(pulled, "row", axis=0, tiled=True)
    grad_links = lax.psum_scatter(
        jnp.dot(pulled_all, factor.T, preferred_element_type=jnp.float32),
        "col",
        scatter_dimension=0,
        tiled=True,
    ).astype(jnp.bfloat16)
    grad_factor = jnp.dot(links_all.T, pulled_all, preferred_element_type=jnp.float32)
    grad_factor = (grad_factor + 2.0 * factor.astype(jnp.float32) * weights[None, :]).astype(
        jnp.bfloat16
    )
    return (grad_root, grad_factor[None], grad_links[None])


def solution(mesh):
    return jax.shard_map(
        local,
        mesh=mesh,
        in_specs=(
            P(("grp", "row"), "col"),
            P("grp", "row", "col"),
            P("grp", "col", "row"),
            P("grp", "col"),
            P("col"),
            P(),
        ),
        out_specs=(P(("grp", "row"), "col"), P("grp", "row", "col"), P("grp", "col", "row")),
        check_vma=False,
    )
```

profile of v0, /device:TPU:0, one launch (start us, length us, event | category | flops | bytes accessed | tf_op | source)
XLA Modules:
  0.0 1300.6 jit_solution(15180582814886838302)
XLA Ops:
  7.2 0.0 all-gather.18.cloned.1.call-start
  7.2 0.7 all-gather.18.cloned.1.call-update
  7.9 0.0 reduce-scatter.5.cloned.1.call-start
  7.9 119.7 %all-gather.18.cloned.1.call-done = bf16[1,1536,2048]{2,1,0:T(8,128)(2,1)} async-done(((bf16[1,384,2048]{2,1,0:T(8,128)(2,1)}), bf16[1,1536,2048]{2,1,0:T(8,128)(2,1)}) %all-gather.18.cloned.1.call-update) | async-done | bytes 6291472 | tf_op jit(solution)/shard_map/all_gather | solution.py:44
  127.7 18.9 %fusion.4 = f32[1536,2048]{1,0:T(8,128)} fusion(bf16[1,2048,2048]{2,1,0:T(8,128)(2,1)} %param.7, bf16[1,1536,2048]{2,1,0:T(8,128)(2,1)} %all-gather.18.cloned.1.call-done), kind=kOutput, calls=%fused_computation.8 | convolution fusion | flops 12884901888 | bytes 27262976 | tf_op jit(solution)/shard_map/dot_general | solution.py:46
  146.6 0.0 all-reduce.2.cloned.1.call-start
  146.7 9.9 copy.24
  156.6 0.5 copy-done.5
  157.1 8.9 convert_bitcast_fusion.1
  166.0 9.0 copy.11
  175.0 8.9 convert_bitcast_fusion
  183.8 8.9 copy.12
  192.7 8.7 pad_maximum_fusion
  201.4 0.0 all-reduce.2.cloned.1.call-update
  201.4 0.0 all-gather.8.cloned.1.call-start
  201.5 64.3 %reduce-scatter.5.cloned.1.call-done = f32[384,2048]{1,0:T(8,128)} async-done(((f32[1536,2048]{1,0:T(8,128)}), f32[384,2048]{1,0:T(8,128)}) %reduce-scatter.5.cloned.1.call-update) | async-done | bytes 3145744 | tf_op jit(solution)/shard_map/reduce_scatter | solution.py:45
  265.7 3.3 convert_element_type.47
  269.0 0.0 all-gather.8.cloned.1.call-update
  269.0 0.3 reduce-scatter.9.cloned.1.call-start
  269.3 324.2 %all-reduce.2.cloned.1.call-done = bf16[1536,2,1536]{0,2,1:T(8,128)(2,1)} async-done(((bf16[1536,2,1536]{0,2,1:T(8,128)(2,1)}), bf16[1536,2,1536]{0,2,1:T(8,128)(2,1)}) %all-reduce.2.cloned.1.call-update) | async-done | bytes 9437200 | tf_op jit(solution)/shard_map/psum | solution.py:29
  593.5 5.3 fusion.12
  598.8 0.1 copy-done.8
  598.9 2.6 fusion.14
  601.6 2.5 pad_maximum_fusion.1
  604.1 0.0 reduce-scatter.9.cloned.1.call-update
  604.1 0.0 reduce-scatter.7.cloned.1.call-start
  604.2 60.7 %all-gather.8.cloned.1.call-done = bf16[1536,2048]{1,0:T(8,128)(2,1)} async-done(((bf16[384,2048]{1,0:T(8,128)(2,1)}), bf16[1536,2048]{1,0:T(8,128)(2,1)}) %all-gather.8.cloned.1.call-update) | async-done | bytes 6291472 | tf_op jit(solution)/shard_map/all_gather | solution.py:51
  664.9 7.7 fusion.20
  672.6 0.0 all-gather.14.cloned.1.call-start
  672.7 50.0 %reduce-scatter.9.cloned.1.call-done = f32[384,384]{1,0:T(8,128)} async-done(((f32[3072,384]{1,0:T(8,128)}), f32[384,384]{1,0:T(8,128)}) %reduce-scatter.9.cloned.1.call-update) | async-done | bytes 589840 | tf_op jit(solution)/shard_map/reduce_scatter | solution.py:38
  722.7 1.8 convert_element_type.52
  724.5 0.0 all-gather.10.cloned.1.call-start
  724.6 49.0 %reduce-scatter.7.cloned.1.call-done = f32[384,384]{1,0:T(8,128)} async-done(((f32[1536,384]{1,0:T(8,128)}), f32[384,384]{1,0:T(8,128)}) %reduce-scatter.7.cloned.1.call-update) | async-done | bytes 589840 | tf_op jit(solution)/shard_map/reduce_scatter | solution.py:53
  773.6 1.8 convert_element_type.50
  775.4 0.0 all-gather.10.cloned.1.call-update
  775.4 0.0 all-gather.16.cloned.1.call-start
  775.5 30.0 %all-gather.14.cloned.1.call-done = bf16[384,1536]{1,0:T(8,128)(2,1)} async-done(((bf16[384,384]{1,0:T(8,128)(2,1)}), bf16[384,1536]{1,0:T(8,128)(2,1)}) %all-gather.14.cloned.1.call-update) | async-done | bytes 1179664 | tf_op jit(solution)/shard_map/all_gather | solution.py:85
  805.5 6.9 multiply_convert_fusion
  812.4 0.0 all-gather.16.cloned.1.call-update
  812.4 0.4 all-gather.12.cloned.1.call-start
  812.9 24.0 %all-gather.10.cloned.1.call-done = bf16[384,3072]{1,0:T(8,128)(2,1)} async-done(((bf16[384,384]{1,0:T(8,128)(2,1)}), bf16[384,3072]{1,0:T(8,128)(2,1)}) %all-gather.10.cloned.1.call-update) | async-done | bytes 2359312 | tf_op jit(solution)/shard_map/all_gather | solution.py:59
  836.9 5.6 reshape.22
  842.5 3.4 fusion.35
  845.9 5.8 fusion.18
  851.7 2.7 fusion.19
  854.4 1.7 pad_maximum_fusion.2
  856.1 0.0 all-gather.12.cloned.1.call-update
  856.1 0.0 reduce-scatter.11.cloned.1.call-start
  856.1 53.5 %all-gather.16.cloned.1.call-done = bf16[1536,2048]{1,0:T(8,128)(2,1)} async-done(((bf16[384,2048]{1,0:T(8,128)(2,1)}), bf16[1536,2048]{1,0:T(8,128)(2,1)}) %all-gather.16.cloned.1.call-update) | async-done | bytes 6291472 | tf_op jit(solution)/shard_map/all_gather | solution.py:89
  909.7 19.2 %fusion.2 = f32[1536,2048]{1,0:T(8,128)} fusion(bf16[1536,2048]{1,0:T(8,128)(2,1)} %all-gather.16.cloned.1.call-done, bf16[1,2048,2048]{2,1,0:T(8,128)(2,1)} %param.7), kind=kOutput, calls=%fused_computation.6 | convolution fusion | flops 12884901888 | bytes 27262976 | tf_op jit(solution)/shard_map/dot_general | solution.py:91
  928.9 0.0 reduce-scatter.11.cloned.1.call-update
  929.0 12.3 copy.13
  941.2 21.1 %fusion.6 = bf16[1,2048,2048]{1,2,0:T(8,128)(2,1)} fusion(f32[2048]{0:T(1024)S(1)} %broadcast_multiply_fusion, bf16[1,2048,2048]{1,2,0:T(8,128)(2,1)} %copy.13, bf16[1536,2048]{1,0:T(8,128)(2,1)} %all-gather.16.cloned.1.call-done, bf16[1,1536,2048]{2,1,0:T(8,128)(2,1)} %all-gather.18.cloned.1.call-done), kind=kOutput, calls=%fused_computation.10 | convolution fusion | flops 12901679104 | bytes 29368320 | tf_op jit(solution)/shard_map/dot_general | solution.py:96
  962.3 12.3 copy.19
  974.6 103.4 %all-gather.12.cloned.1.call-done = bf16[1536,2,1536]{2,0,1:T(8,128)(2,1)} async-done(((bf16[1536,2,384]{2,0,1:T(8,128)(2,1)}), bf16[1536,2,1536]{2,0,1:T(8,128)(2,1)}) %all-gather.12.cloned.1.call-update) | async-done | bytes 9437200 | tf_op jit(solution)/shard_map/all_gather | solution.py:73
  1078.0 12.6 copy.16
  1090.6 8.4 fusion.34
  1099.1 9.1 copy.23
  1108.2 9.2 copy.22
  1117.5 10.5 fusion.8
  1128.0 16.0 %add_multiply_fusion = f32[24,1536,128]{2,0,1:T(8,128)} fusion(f32[24,1536,128]{2,0,1:T(8,128)} %fusion.8, bf16[1536,1,12,128]{3,2,0,1:T(8,128)(2,1)} %copy.23, s32[12]{0:T(128)S(1)} %copy-done.4), kind=kOutput, calls=%fused_computation.2 | convolution fusion | flops 122683680 | bytes 42467376 | tf_op jit(solution)/shard_map/rjb,jk->rkb/dot_general | solution.py:79
  1144.0 14.5 %fusion = bf16[1536,3072]{1,0:T(8,128)(2,1)} fusion(f32[192,8,24,128]{3,2,1,0:T(8,128)} %bitcast.100, bf16[1536,3072]{1,0:T(8,128)(2,1)S(1)} %bitcast.104, f32[3072]{0:T(1024)S(1)} %convert_multiply_fusion), kind=kLoop, calls=%fused_computation.1 | loop fusion | flops 18874368 | bytes 37761024 | tf_op jit(solution)/shard_map/convert_element_type | solution.py:82
  1158.5 132.1 %reduce-scatter.11.cloned.1.call-done = f32[384,2048]{1,0:T(8,128)} async-done(((f32[1536,2048]{1,0:T(8,128)}), f32[384,2048]{1,0:T(8,128)}) %reduce-scatter.11.cloned.1.call-update) | async-done | bytes 3145744 | tf_op jit(solution)/shard_map/reduce_scatter | solution.py:90
  1290.6 3.3 convert_bitcast_fusion.2
  (38 shorter events, 0.1 us)
Async XLA Ops:
  7.2 120.5 %all-gather.18.cloned.1.call-start = ((), (), s32[]{:S(2)}) async-start(), calls=%async_computation.14 | async-start | bytes 7864320 | tf_op jit(solution)/shard_map/all_gather | solution.py:44
  7.9 257.8 %reduce-scatter.5.cloned.1.call-start = ((), (), s32[]{:S(2)}) async-start(), calls=%async_computation.5 | async-start | bytes 15728640 | tf_op jit(solution)/shard_map/reduce_scatter | solution.py:45
  146.6 446.8 %all-reduce.2.cloned.1.call-start = ((), (), s32[]{:S(2)}) async-start(), calls=%async_computation.4 | async-start | bytes 18874368 | tf_op jit(solution)/shard_map/psum | solution.py:29
  146.7 9.9 copy-start.7
  156.6 0.5 copy-start.5
  156.6 18.4 %copy-start.3 = (s32[12]{0:T(128)}, s32[12]{0:T(128)S(1)}, u32[]{:S(2)}) copy-start(s32[12]{0:T(128)S(1)} %get-tuple-element.14) | copy-start | bytes 148
  201.4 463.5 %all-gather.8.cloned.1.call-start = ((), (), s32[]{:S(2)}) async-start(), calls=%async_computation.6 | async-start | bytes 7864320 | tf_op jit(solution)/shard_map/all_gather | solution.py:51
  269.0 453.7 %reduce-scatter.9.cloned.1.call-start = ((), (), s32[]{:S(2)}) async-start(), calls=%async_computation.10 | async-start | bytes 5308416 | tf_op jit(solution)/shard_map/reduce_scatter | solution.py:38
  593.5 5.4 copy-start.8
  601.5 2.6 copy-start.1
  601.5 63.4 %copy-start = (bf16[384,2048]{1,0:T(8,128)(2,1)S(1)}, bf16[384,2048]{1,0:T(8,128)(2,1)}, u32[]{:S(2)}) copy-start(bf16[384,2048]{1,0:T(8,128)(2,1)} %convert_element_type.47) | copy-start | bytes 4718596
  604.1 169.5 %reduce-scatter.7.cloned.1.call-start = ((), (), s32[]{:S(2)}) async-start(), calls=%async_computation.7 | async-start | bytes 2949120 | tf_op jit(solution)/shard_map/reduce_scatter | solution.py:53
  672.6 132.9 %all-gather.14.cloned.1.call-start = ((), (), s32[]{:S(2)}) async-start(), calls=%async_computation.11 | async-start | bytes 1474560 | tf_op jit(solution)/shard_map/all_gather | solution.py:85
  724.5 112.4 %all-gather.10.cloned.1.call-start = ((), (), s32[]{:S(2)}) async-start(), calls=%async_computation.8 | async-start | bytes 2654208 | tf_op jit(solution)/shard_map/all_gather | solution.py:59
  775.4 134.3 %all-gather.16.cloned.1.call-start = ((), (), s32[]{:S(2)}) async-start(), calls=%async_computation.12 | async-start | bytes 7864320 | tf_op jit(solution)/shard_map/all_gather | solution.py:89
  812.4 265.6 %all-gather.12.cloned.1.call-start = ((), (), s32[]{:S(2)}) async-start(), calls=%async_computation.9 | async-start | bytes 11796480 | tf_op jit(solution)/shard_map/all_gather | solution.py:73
  842.5 9.2 slice-start.3
  842.5 9.2 slice-start.4
  845.9 5.8 slice-start.5
  856.1 434.5 %reduce-scatter.11.cloned.1.call-start = ((), (), s32[]{:S(2)}) async-start(), calls=%async_computation.13 | async-start | bytes 15728640 | tf_op jit(solution)/shard_map/reduce_scatter | solution.py:90
  929.0 12.3 copy-start.2
  1108.2 9.2 copy-start.6
  1117.4 10.6 copy-start.4
  1117.5 26.5 %slice-start = ((s8[9437184]{0:T(1024)(128)(4,1)}), s8[4194304]{0:T(1024)(128)(4,1)S(1)}, s32[]{:S(2)}) async-start(s8[9437184]{0:T(1024)(128)(4,1)} %bitcast.103), calls=%async_computation.15 | async-start | bytes 8388608
  1117.5 26.5 %slice-start.1 = ((s8[9437184]{0:T(1024)(128)(4,1)}), s8[4194304]{0:T(1024)(128)(4,1)S(1)}, s32[]{:S(2)}) async-start(s8[9437184]{0:T(1024)(128)(4,1)} %bitcast.103), calls=%async_computation.16 | async-start | bytes 8388608
  1128.0 16.0 %slice-start.2 = ((s8[9437184]{0:T(1024)(128)(4,1)}), s8[1048576]{0:T(1024)(128)(4,1)S(1)}, s32[]{:S(2)}) async-start(s8[9437184]{0:T(1024)(128)(4,1)} %bitcast.103), calls=%async_computation.17 | async-start | bytes 2097152
Sparse Core Ops, SparseCore 0:
  9.6 118.0 all-gather.17
  146.7 118.9 reduce-scatter.4
  268.8 324.6 all-reduce.1
  595.7 69.1 all-gather.7
  668.8 53.8 reduce-scatter.8
  725.5 48.0 reduce-scatter.6
  775.9 29.5 all-gather.13
  808.1 28.7 all-gather.9
  839.5 70.1 all-gather.15
  911.2 166.7 all-gather.11
  1080.5 210.0 reduce-scatter.10
where the time goes:
time: 1310 us; the launch traced here: 1300 us
  waiting for transfers between devices  1010 us (77%)
  matrix products  134 us (10%)
  local copies, waits for them, and re-layouts  101 us (8%)
  other arithmetic  37.5 us (3%)
  between operations  14.3 us (1%)
    psum x1, waiting for transfers between devices, local(): selected = lax.psum(picked.astype(jnp.bfloat16), 'col')  324 us
    reduce_scatter x1, waiting for transfers between devices, local(): lax.psum_scatter(jnp.dot(pulled_all, factor.T, preferred_element_type=jnp...  132 us
    all_gather x1, waiting for transfers between devices, local(): links_all = lax.all_gather(links, 'col', axis=0, tiled=True)  120 us
    all_gather x1, waiting for transfers between devices, local(): lax.all_gather(lifted, 'col', axis=2, tiled=True)  103 us
    reduce_scatter x1, waiting for transfers between devices, local(): lax.psum_scatter(jnp.dot(links_all, factor, preferred_element_type=jnp.fl...  64.3 us
    all_gather x1, waiting for transfers between devices, local(): solved_all = lax.all_gather(solved, 'row', axis=0, tiled=True)  60.7 us
    all_gather x1, waiting for transfers between devices, local(): pulled_all = lax.all_gather(pulled, 'row', axis=0, tiled=True)  53.5 us
    unnamed x35, local copies, waits for them, and re-layouts  53.5 us
  transfers between devices with their start and end apart: 11, of which 11 were waited for; matrix products, arithmetic and copies ran while one was open for 19% of the time, Pallas kernels for 0%

commit v1 on v0

v1 whole, which is shorter than its diff:
```python
import functools

import jax
import jax.numpy as jnp
from jax import lax
from jax.experimental import pallas as pl
from jax.experimental.pallas import tpu as pltpu
from jax.sharding import PartitionSpec as P

BW = 128
F32 = jnp.float32
BF16 = jnp.bfloat16


def mm(a, b, contract):
    return lax.dot_general(a, b, (contract, ((), ())), preferred_element_type=F32)


def pick_kernel(place, owned, root_ref, out_ref):
    s = pl.program_id(0)

    @pl.when(owned[s] == 1)
    def _():
        out_ref[...] = root_ref[...]

    @pl.when(owned[s] == 0)
    def _():
        out_ref[...] = jnp.zeros_like(out_ref)


def pick(root, place, owned):
    rows, slots = root.shape[0], place.shape[0]
    return pl.pallas_call(
        pick_kernel,
        grid_spec=pltpu.PrefetchScalarGridSpec(
            num_scalar_prefetch=2,
            grid=(slots,),
            in_specs=[pl.BlockSpec((rows, BW), lambda s, place, owned: (0, place[s]))],
            out_specs=pl.BlockSpec((rows, BW), lambda s, place, owned: (0, s)),
        ),
        out_shape=jax.ShapeDtypeStruct((rows, slots * BW), BF16),
        cost_estimate=pl.CostEstimate(
            flops=0, bytes_accessed=2 * rows * slots * BW * 2, transcendentals=0
        ),
    )(place, owned, root)


def finish_kernel(
    share,
    at,
    has,
    spot,
    root_ref,
    weight_ref,
    mine_ref,
    other_ref,
    s0,
    s1,
    s2,
    s3,
    out_ref,
):
    block = pl.program_id(0)
    width = mine_ref.shape[0]
    out_ref[...] = (2.0 * root_ref[...].astype(F32) * weight_ref[...].astype(F32)).astype(BF16)

    @pl.when(has[0, block] + has[1, block] > 0)
    def _():
        scale = weight_ref[...].astype(F32)
        for index, part in enumerate((s0, s1, s2, s3)):
            start = pl.multiple_of(spot[index] * share, share)
            rows = pl.ds(start, share)
            out = 2.0 * root_ref[rows, :].astype(F32) * scale
            for which, adjoint in enumerate((mine_ref, other_ref)):
                column = pl.multiple_of(spot[4 + which] * width, BW)
                lifted = jnp.dot(
                    part[:, pl.ds(column, width)], adjoint[...], preferred_element_type=F32
                ).astype(BF16)
                keep = jnp.where(has[which, block] == 1, 2.0, 0.0).astype(F32)
                out = out + keep * lifted.astype(F32)
            out_ref[rows, :] = out.astype(BF16)


def finish(root, weights, mine, other, parts, at, has, spot):
    rows, columns = root.shape
    blocks = columns // BW
    width = mine.shape[0]
    share = parts[0].shape[0]
    whole = pl.BlockSpec(parts[0].shape, lambda b, at, has, spot: (0, 0))
    return pl.pallas_call(
        functools.partial(finish_kernel, share),
        grid_spec=pltpu.PrefetchScalarGridSpec(
            num_scalar_prefetch=3,
            grid=(blocks,),
            in_specs=[
                pl.BlockSpec((rows, BW), lambda b, at, has, spot: (0, b)),
                pl.BlockSpec((1, BW), lambda b, at, has, spot: (0, b)),
                pl.BlockSpec((width, BW), lambda b, at, has, spot: (0, at[0, b])),
                pl.BlockSpec((width, BW), lambda b, at, has, spot: (0, at[1, b])),
                whole,
                whole,
                whole,
                whole,
            ],
            out_specs=pl.BlockSpec((rows, BW), lambda b, at, has, spot: (0, b)),
        ),
        out_shape=jax.ShapeDtypeStruct((rows, columns), BF16),
        compiler_params=pltpu.CompilerParams(vmem_limit_bytes=48 * 2**20),
        cost_estimate=pl.CostEstimate(
            flops=2 * rows * width * width,
            bytes_accessed=2 * rows * (2 * columns + 2 * width) * 2,
            transcendentals=0,
        ),
    )(at, has, spot, root, weights, mine, other, *parts)


def swap(x, axis, d):
    n = lax.axis_size(axis)
    return lax.ppermute(x, axis, [(i, i ^ d) for i in range(n)])


FAR, MIDDLE, NEAR = (3, 3, 0, 0), (2, 2, 1, 1), (1, 0, 3, 2)


def up(x, lo, hi):
    return lax.ppermute(x, "col", [(i, i + 1) for i in range(lo, hi + 1)])


def down(x, lo, hi):
    return lax.ppermute(x, "col", [(i, i - 1) for i in range(lo, hi + 1)])


def line_gather(x, z):
    up1, down1 = up(x, 0, 2), down(x, 1, 3)
    near = jnp.where(z % 2 == 0, down1, up1)
    up2, down2 = up(up1, 1, 2), down(down1, 1, 2)
    middle = jnp.where(z < 2, jnp.where(z == 0, down2, down1), jnp.where(z == 2, up1, up2))
    up3, down3 = up(up2, 2, 2), down(down2, 1, 1)
    far = jnp.where(z < 2, jnp.where(z == 0, down3, down2), jnp.where(z == 2, up2, up3))
    return [far, middle, near, x]


def line_scatter(chunks, z, join):
    far, middle, near, own = chunks
    up1, down1 = up(far, 0, 0), down(far, 3, 3)
    up2 = up(join(jnp.where(z == 0, middle, far), up1), 0, 1)
    down2 = down(join(jnp.where(z == 3, middle, far), down1), 2, 3)
    up3 = up(join(jnp.where(z == 1, middle, near), up2), 0, 2)
    down3 = down(join(jnp.where(z == 2, middle, near), down2), 1, 3)
    return join(join(own, up3), down3)


def add(a, b):
    return (a.astype(F32) + b.astype(F32)).astype(BF16)


def row_scatter(chunk, r, n):
    if n != 4:
        parts = jnp.stack([chunk(i).astype(BF16) for i in range(n)])
        return lax.psum_scatter(parts, "row", scatter_dimension=0, tiled=False).astype(F32)
    arrived = [swap(chunk(r ^ d).astype(BF16), "row", d) for d in (1, 2, 3)]
    return sum((a.astype(F32) for a in arrived), chunk(r).astype(F32))


def row_gather(x, r, n, axis):
    if n != 4:
        return lax.all_gather(x, "row", axis=axis, tiled=True)
    shape = list(x.shape)
    step = shape[axis]
    shape[axis] = step * n
    whole = jnp.zeros(shape, x.dtype)
    for d in range(n):
        piece = swap(x, "row", d) if d else x
        whole = lax.dynamic_update_slice_in_dim(whole, piece, (r ^ d) * step, axis)
    return whole


def col_sum(x, z):
    n = lax.axis_size("col")
    step = x.shape[0] // n
    piece = lambda i: lax.dynamic_slice_in_dim(x, i * step, step, 0)
    arrived = [swap(piece(z ^ d).astype(BF16), "col", d) for d in range(1, n)]
    total = sum((a.astype(F32) for a in arrived), piece(z)).astype(BF16)
    whole = jnp.zeros(x.shape, BF16)
    for d in range(n):
        part = swap(total, "col", d) if d else total
        whole = lax.dynamic_update_slice_in_dim(whole, part, (z ^ d) * step, 0)
    return whole


def local(root, child_inverse, coupling, child_weights, root_weights, parent_blocks):
    g, r, z = lax.axis_index("grp"), lax.axis_index("row"), lax.axis_index("col")
    nrow, ncol = lax.axis_size("row"), lax.axis_size("col")
    root_rows, root_cols = root.shape
    blocks = root_cols // BW
    factor, links = child_inverse[0], coupling[0]
    weights = child_weights[0].astype(F32)
    share = links.shape[0]
    width = share * ncol
    count = width // BW
    cols = factor.shape[1]
    sub = cols // nrow
    strip = width // nrow
    order = [jnp.array(t, jnp.int32)[z] for t in (FAR, MIDDLE, NEAR)] + [z]

    offset = parent_blocks.reshape(-1) - z * blocks
    owned = (offset >= 0) & (offset < blocks)
    picked = pick(root, jnp.clip(offset, 0, blocks - 1), owned.astype(jnp.int32))
    band = root_rows // ncol
    rows_of = lambda q: lax.dynamic_slice_in_dim(picked, q * band, band, 0)
    selected = line_scatter([rows_of(q) for q in order], z, jnp.add)

    mine = lax.dynamic_slice_in_dim(selected, g * width, width, 1)
    other = lax.dynamic_slice_in_dim(selected, (1 - g) * width, width, 1)
    theirs = swap(mm(other, other, ((0,), (0,))).astype(BF16), "grp", 1)

    def margin_rows(i):
        left = lax.dynamic_slice_in_dim(mine, i * strip, strip, 1)
        there = lax.dynamic_slice_in_dim(theirs, i * strip, strip, 0)
        return mm(left, mine, ((0,), (0,))) + there.astype(F32)

    margin = row_gather(col_sum(row_scatter(margin_rows, r, nrow), z), r, nrow, 0)

    links_parts = line_gather(links, z)
    solved = jnp.zeros((width, sub), BF16)
    for q, part in zip(reversed(order), reversed(links_parts)):
        product = mm(part, factor, ((1,), (0,)))
        piece = row_scatter(
            lambda i: lax.dynamic_slice_in_dim(product, i * sub, sub, 1), r, nrow
        ).astype(BF16)
        solved = lax.dynamic_update_slice_in_dim(solved, piece, q * share, 0)
    my_weights = lax.dynamic_slice_in_dim(weights, r * sub, sub, 0)[None, :]
    scaled = (solved.astype(F32) * my_weights).astype(BF16)

    pulled_parts, partial = [], []
    for q in order:
        left = lax.dynamic_slice_in_dim(margin, q * share, share, 0)
        pulled = (2.0 * mm(left, solved, ((1,), (0,))) * my_weights).astype(BF16)
        pulled = row_gather(pulled, r, nrow, 1)
        pulled_parts.append(pulled)
        partial.append(mm(pulled, factor, ((1,), (1,))).astype(BF16))
    grad_links = line_scatter(partial, z, add)

    def adjoint_rows(i):
        return mm(lax.dynamic_slice_in_dim(scaled, i * strip, strip, 0), solved, ((1,), (1,)))

    adjoint = row_gather(col_sum(row_scatter(adjoint_rows, r, nrow), z), r, nrow, 0)
    adjoint_other = swap(adjoint, "grp", 1)

    grad_factor = mm(
        jnp.concatenate(links_parts, axis=0),
        jnp.concatenate(pulled_parts, axis=0),
        ((0,), (0,)),
    )
    grad_factor = (grad_factor + 2.0 * factor.astype(F32) * weights[None, :]).astype(BF16)

    parts = line_gather(selected, z)
    offset = offset.reshape(2, count)
    children = jnp.stack([g, 1 - g])
    match = offset[children][:, :, None] == jnp.arange(blocks, dtype=jnp.int32)[None, None, :]
    has = jnp.any(match, axis=1).astype(jnp.int32)
    at = jnp.argmax(match, axis=1).astype(jnp.int32)
    spot = jnp.stack(order + [g, 1 - g]).astype(jnp.int32)
    grad_root = finish(root, root_weights[None, :], adjoint, adjoint_other, parts, at, has, spot)
    return (grad_root, grad_factor[None], grad_links[None])


def solution(mesh):
    return jax.shard_map(
        local,
        mesh=mesh,
        in_specs=(
            P(("grp", "row"), "col"),
            P("grp", "row", "col"),
            P("grp", "col", "row"),
            P("grp", "col"),
            P("col"),
            P(),
        ),
        out_specs=(P(("grp", "row"), "col"), P("grp", "row", "col"), P("grp", "col", "row")),
        check_vma=False,
    )
```

time: 1310 us -> 847 us (0.65)
  waiting for transfers between devices: 1010 us -> 429 us
  starting transfers between devices: 1.07 us -> 176 us
  local copies, waits for them, and re-layouts: 101 us -> 30.7 us
  Pallas kernels: 0 us -> 60.5 us
  matrix products: 134 us -> 95.9 us
    ppermute x0 -> x74, waiting for transfers between devices: none -> 429 us  [the longest x50 321 us: swap(): return lax.ppermute(x, axis, [(i, i ^ d) for i in range(n)])]
    all_gather x6 -> x0, waiting for transfers between devices: 391 us -> none  [the longest x1 120 us: local(): links_all = lax.all_gather(links, 'col', axis=0, tiled=True)]
    psum x1 -> x0, waiting for transfers between devices: 324 us -> none  [local(): selected = lax.psum(picked.astype(jnp.bfloat16), 'col')]
    reduce_scatter x4 -> x0, waiting for transfers between devices: 295 us -> none  [the longest x1 132 us: local(): lax.psum_scatter(jnp.dot(pulled_all, factor.T, preferred_element_type=jnp...]
    ppermute x0 -> x74, starting transfers between devices: none -> 176 us  [the longest x50 85.1 us: swap(): return lax.ppermute(x, axis, [(i, i ^ d) for i in range(n)])]
    pallas_call x0 -> x2, Pallas kernels: none -> 60.5 us  [the longest x1 44.9 us: finish(): pl.pallas_call(functools.partial(finish_kernel, share), grid_spec=pltpu.P...]
    unnamed x35 -> x44, local copies, waits for them, and re-layouts: 53.5 us -> 7.51 us
    dot_general x13 -> x22, matrix products: 134 us -> 95.9 us  [mm(): lax.dot_general(a, b, (contract, ((), ())), preferred_element_type=F32)]
  transfers between devices with their start and end apart: 11 -> 74, of which waited for: 11 -> 34; matrix products, arithmetic and copies ran while one was open for 19% -> 18% of each run, Pallas kernels for 0% -> 5%
where the time goes in v1:
time: 847 us; the launch traced here: 838 us
  waiting for transfers between devices  429 us (51%)
  starting transfers between devices  176 us (21%)
  matrix products  95.9 us (11%)
  Pallas kernels  60.5 us (7%)
  other arithmetic  42 us (5%)
  local copies, waits for them, and re-layouts  30.7 us (4%)
    ppermute x50, waiting for transfers between devices, swap(): return lax.ppermute(x, axis, [(i, i ^ d) for i in range(n)])  321 us
    dot_general x22, matrix products, mm(): lax.dot_general(a, b, (contract, ((), ())), preferred_element_type=F32)  95.9 us
    ppermute x50, starting transfers between devices, swap(): return lax.ppermute(x, axis, [(i, i ^ d) for i in range(n)])  85.1 us
    ppermute x12, waiting for transfers between devices, up(): return lax.ppermute(x, 'col', [(i, i + 1) for i in range(lo, hi + 1)])  77.3 us
    ppermute x12, starting transfers between devices, up(): return lax.ppermute(x, 'col', [(i, i + 1) for i in range(lo, hi + 1)])  74.5 us
    pallas_call x1, Pallas kernels, finish(): pl.pallas_call(functools.partial(finish_kernel, share), grid_spec=pltpu.P...  44.9 us
    ppermute x12, waiting for transfers between devices, down(): return lax.ppermute(x, 'col', [(i, i - 1) for i in range(lo, hi + 1)])  29.9 us
  transfers between devices with their start and end apart: 74, of which 34 were waited for; matrix products, arithmetic and copies ran while one was open for 18% of the time, Pallas kernels for 5%

profile of v1, /device:TPU:0, one launch (start us, length us, event | category | flops | bytes accessed | tf_op | source)
XLA Modules:
  0.0 838.1 jit_solution(6389272987418903781)
XLA Ops:
  4.5 15.7 %shard_map.112 = bf16[1536,3072]{1,0:T(8,128)(2,1)} custom-call(s32[24]{0:T(128)} %min.12.place, s32[24]{0:T(128)} %reshape.117.owned, bf16[1536,3072]{1,0:T(8,128)(2,1)} %root_ref.3), custom_call_target="tpu_custom_call" | custom-call | bytes 18874368 | tf_op jit(solution)/shard_map/pallas_call | solution.py:33
  22.0 7.0 collective-permute-start.31
  32.3 5.7 collective-permute-start.4
  39.2 29.9 %collective-permute-done.3 = bf16[384,2048]{1,0:T(8,128)(2,1)} collective-permute-done((bf16[384,2048]{1,0:T(8,128)(2,1)}, bf16[384,2048]{1,0:T(8,128)(2,1)}, u32[]{:S(2)}, u32[]{:S(2)}) %collective-permute-start.3) | collective-permute-done | bytes 1572896 | tf_op jit(solution)/shard_map/ppermute | solution.py:130
  70.4 41.4 %collective-permute-done.4 = bf16[384,2048]{1,0:T(8,128)(2,1)} collective-permute-done((bf16[384,2048]{1,0:T(8,128)(2,1)}, bf16[384,2048]{1,0:T(8,128)(2,1)}, u32[]{:S(2)}, u32[]{:S(2)}) %collective-permute-start.4) | collective-permute-done | bytes 1572896 | tf_op jit(solution)/shard_map/ppermute | solution.py:126
  113.6 8.1 select_add_fusion.2
  121.7 11.9 %collective-permute-start.32 = (bf16[384,3072]{1,0:T(8,128)(2,1)}, bf16[384,3072]{1,0:T(8,128)(2,1)S(1)}, u32[]{:S(2)}, u32[]{:S(2)}) collective-permute-start(bf16[384,3072]{1,0:T(8,128)(2,1)} %get-tuple-element.11), channel_id=1, source_target_pairs={{0,1},{1,2},{4,5},{5,6},{8,9},{9,10},{12,13},{13,14},{16,17},{17,1... | collective-permute-start | bytes 7077896 | tf_op jit(solution)/shard_map/ppermute | solution.py:126
  135.7 6.3 fusion.14
  145.3 7.9 collective-permute-done
  158.0 3.8 collective-permute-done.1
  166.9 3.7 collective-permute-done.2
  172.1 10.9 %collective-permute-done.32 = bf16[384,3072]{1,0:T(8,128)(2,1)S(1)} collective-permute-done((bf16[384,3072]{1,0:T(8,128)(2,1)}, bf16[384,3072]{1,0:T(8,128)(2,1)S(1)}, u32[]{:S(2)}, u32[]{:S(2)}) %collective-permute-start.32) | collective-permute-done | bytes 2359328 | tf_op jit(solution)/shard_map/ppermute | solution.py:126
  183.1 5.3 select_add_fusion.3
  188.4 25.2 %collective-permute-start.33 = (bf16[384,3072]{1,0:T(8,128)(2,1)S(1)}, bf16[384,3072]{1,0:T(8,128)(2,1)S(1)}, u32[]{:S(2)}, u32[]{:S(2)}) collective-permute-start(bf16[384,3072]{1,0:T(8,128)(2,1)S(1)} %get-tuple-element.13), channel_id=1, source_target_pairs={{0,1},{1,2},{2,3},{4,5},{5,6},{6,7},{8,9},{9,10},{10,11},{12,13},{... | collective-permute-start | bytes 7077896 | tf_op jit(solution)/shard_map/ppermute | solution.py:126
  215.1 4.2 select_select_fusion.2
  219.4 3.5 fusion.12
  226.6 3.5 fusion.10
  230.3 4.9 collective-permute-done.5
  236.6 5.6 collective-permute-done.6
  246.0 3.5 fusion.8
  253.5 8.5 %collective-permute-done.11 = bf16[384,512]{1,0:T(8,128)(2,1)S(1)} collective-permute-done((bf16[384,512]{1,0:T(8,128)(2,1)S(1)}, bf16[384,512]{1,0:T(8,128)(2,1)S(1)}, u32[]{:S(2)}, u32[]{:S(2)}) %collective-permute-start.11) | collective-permute-done | bytes 393248 | tf_op jit(solution)/shard_map/ppermute | solution.py:119
  264.0 4.9 collective-permute-done.15
  269.0 8.2 collective-permute-done.16
  282.8 3.3 add_add_fusion.s3
  286.1 4.3 convolution_convert_fusion
  295.7 13.0 %collective-permute-done.18 = bf16[384,1536]{1,0:T(8,128)(2,1)S(1)} collective-permute-done((bf16[384,1536]{1,0:T(8,128)(2,1)}, bf16[384,1536]{1,0:T(8,128)(2,1)S(1)}, u32[]{:S(2)}, u32[]{:S(2)}) %collective-permute-start.18) | collective-permute-done | bytes 1179680 | tf_op jit(solution)/shard_map/ppermute | solution.py:119
  308.7 22.3 %collective-permute-done.19 = bf16[384,1536]{1,0:T(8,128)(2,1)} collective-permute-done((bf16[384,1536]{1,0:T(8,128)(2,1)}, bf16[384,1536]{1,0:T(8,128)(2,1)}, u32[]{:S(2)}, u32[]{:S(2)}) %collective-permute-start.19) | collective-permute-done | bytes 1179680 | tf_op jit(solution)/shard_map/ppermute | solution.py:119
  331.0 3.2 fusion.35
  341.2 21.8 %collective-permute-done.21 = bf16[96,1536]{1,0:T(8,128)(2,1)S(1)} collective-permute-done((bf16[96,1536]{1,0:T(8,128)(2,1)}, bf16[96,1536]{1,0:T(8,128)(2,1)S(1)}, u32[]{:S(2)}, u32[]{:S(2)}) %collective-permute-start.21) | collective-permute-done | bytes 294944 | tf_op jit(solution)/shard_map/ppermute | solution.py:119
  366.8 4.6 collective-permute-done.23
  373.0 6.2 collective-permute-start.24
  379.2 43.4 %collective-permute-done.24 = bf16[96,1536]{1,0:T(8,128)(2,1)S(1)} collective-permute-done((bf16[96,1536]{1,0:T(8,128)(2,1)S(1)}, bf16[96,1536]{1,0:T(8,128)(2,1)S(1)}, u32[]{:S(2)}, u32[]{:S(2)}) %collective-permute-start.24) | collective-permute-done | bytes 294944 | tf_op jit(solution)/shard_map/ppermute | solution.py:119
  422.6 3.5 collective-permute-start.26
  429.0 5.0 collective-permute-done.26
  443.1 3.2 fusion.37
  446.3 16.8 %collective-permute-done.27 = bf16[384,1536]{1,0:T(8,128)(2,1)} collective-permute-done((bf16[384,1536]{1,0:T(8,128)(2,1)S(1)}, bf16[384,1536]{1,0:T(8,128)(2,1)}, u32[]{:S(2)}, u32[]{:S(2)}) %collective-permute-start.27) | collective-permute-done | bytes 1179680 | tf_op jit(solution)/shard_map/ppermute | solution.py:119
  467.6 21.3 %collective-permute-done.29 = bf16[384,1536]{1,0:T(8,128)(2,1)} collective-permute-done((bf16[384,1536]{1,0:T(8,128)(2,1)S(1)}, bf16[384,1536]{1,0:T(8,128)(2,1)}, u32[]{:S(2)}, u32[]{:S(2)}) %collective-permute-start.29) | collective-permute-done | bytes 1179680 | tf_op jit(solution)/shard_map/ppermute | solution.py:119
  500.4 13.3 %collective-permute-done.44 = bf16[384,1536]{1,0:T(8,128)(2,1)} collective-permute-done((bf16[384,1536]{1,0:T(8,128)(2,1)S(1)}, bf16[384,1536]{1,0:T(8,128)(2,1)}, u32[]{:S(2)}, u32[]{:S(2)}) %collective-permute-start.44) | collective-permute-done | bytes 1179680 | tf_op jit(solution)/shard_map/ppermute | solution.py:119
  514.0 23.2 %collective-permute-done.46 = bf16[384,1536]{1,0:T(8,128)(2,1)} collective-permute-done((bf16[384,1536]{1,0:T(8,128)(2,1)}, bf16[384,1536]{1,0:T(8,128)(2,1)}, u32[]{:S(2)}, u32[]{:S(2)}) %collective-permute-start.46) | collective-permute-done | bytes 1179680 | tf_op jit(solution)/shard_map/ppermute | solution.py:119
  537.2 3.6 fusion.33
  542.3 7.9 collective-permute-start.47
  553.8 5.9 collective-permute-start.48
  559.8 3.3 collective-permute-start.49
  563.7 14.5 %collective-permute-done.48 = bf16[96,1536]{1,0:T(8,128)(2,1)S(1)} collective-permute-done((bf16[96,1536]{1,0:T(8,128)(2,1)S(1)}, bf16[96,1536]{1,0:T(8,128)(2,1)S(1)}, u32[]{:S(2)}, u32[]{:S(2)}) %collective-permute-start.48) | collective-permute-done | bytes 294944 | tf_op jit(solution)/shard_map/ppermute | solution.py:119
  579.5 6.4 collective-permute-start.50
  588.4 43.4 %collective-permute-done.50 = bf16[96,1536]{1,0:T(8,128)(2,1)S(1)} collective-permute-done((bf16[96,1536]{1,0:T(8,128)(2,1)S(1)}, bf16[96,1536]{1,0:T(8,128)(2,1)S(1)}, u32[]{:S(2)}, u32[]{:S(2)}) %collective-permute-start.50) | collective-permute-done | bytes 294944 | tf_op jit(solution)/shard_map/ppermute | solution.py:119
  631.8 3.4 collective-permute-start.52
  635.2 6.7 collective-permute-done.52
  646.0 6.9 broadcast_select_fusion
  653.0 44.9 %shard_map.113 = bf16[1536,3072]{1,0:T(8,128)(2,1)} custom-call(s32[2,24]{1,0:T(2,128)S(1)} %get-tuple-element.4.at, s32[2,24]{1,0:T(2,128)S(1)} %convert_element_type.280.has, s32[6]{0:T(128)S(1)} %stack.27.spot, bf16[1536,3072]{1,0:T(8,128)(2,1)} %root_ref.3, bf16[1,3072]{1,0:T(2,128)(2,1)S(1)} %broadcast_in_dim.8.weight_ref, ...), custom_call_target="tpu_custom_call" | custom-call | flops 7247757312 | bytes 56623104 | tf_op jit(solution)/shard_map/pallas_call | solution.py:90
  707.5 4.9 collective-permute-done.56
  713.5 7.5 collective-permute-done.57
  722.5 6.8 fusion.48
  729.3 3.4 collective-permute-start.68
  739.1 7.4 fusion.42
  746.5 13.7 %collective-permute-done.68 = bf16[384,2048]{1,0:T(8,128)(2,1)S(1)} collective-permute-done((bf16[384,2048]{1,0:T(8,128)(2,1)S(1)}, bf16[384,2048]{1,0:T(8,128)(2,1)S(1)}, u32[]{:S(2)}, u32[]{:S(2)}) %collective-permute-start.68) | collective-permute-done | bytes 1572896 | tf_op jit(solution)/shard_map/ppermute | solution.py:126
  763.0 4.5 collective-permute-start.69
  771.0 6.1 collective-permute-done.67
  777.1 7.4 fusion.45
  784.5 11.2 %collective-permute-done.69 = bf16[384,2048]{1,0:T(8,128)(2,1)S(1)} collective-permute-done((bf16[384,2048]{1,0:T(8,128)(2,1)S(1)}, bf16[384,2048]{1,0:T(8,128)(2,1)S(1)}, u32[]{:S(2)}, u32[]{:S(2)}) %collective-permute-start.69) | collective-permute-done | bytes 1572896 | tf_op jit(solution)/shard_map/ppermute | solution.py:126
  797.2 5.8 collective-permute-start.70
  804.6 21.9 %fusion.16 = bf16[1,2048,2048]{2,1,0:T(8,128)(2,1)} fusion(f32[2048]{0:T(1024)S(1)} %bitcast.64, bf16[1,2048,2048]{2,1,0:T(8,128)(2,1)} %param.10, bf16[384,2048]{1,0:T(8,128)(2,1)} %bitcast.6, bf16[384,2048]{1,0:T(8,128)(2,1)} %copy-done.12, bf16[384,2048]{1,0:T(8,128)(2,1)} %copy-done.11, bf16[384,2048]{1,0:T(8,128)(2,1)} %copy-done.10, ...), kind=kOutput, calls=%fused_computation.19 | convolution fusion | flops 12952010752 | bytes 29368320 | tf_op jit(solution)/shard_map/dot_general | solution.py:16
  826.5 7.3 fusion.39
  833.8 3.9 fusion.51
  (229 shorter events, 137.9 us)
Async XLA Ops:
  22.0 91.6 %collective-permute-start.31 = (bf16[384,3072]{1,0:T(8,128)(2,1)S(1)}, bf16[384,3072]{1,0:T(8,128)(2,1)}, u32[]{:S(2)}, u32[]{:S(2)}) collective-permute-start(bf16[384,3072]{1,0:T(8,128)(2,1)S(1)} %constant_dynamic-slice_fusion), channel_id=1, source_target_pairs={{0,1},{4,5},{8,9},{12,13},{16,17},{20,21},{24,25},{28,29}} | collective-permute-start | bytes 7077896 | tf_op jit(solution)/shard_map/ppermute | solution.py:126
  29.0 84.6 %collective-permute-start.34 = (bf16[384,3072]{1,0:T(8,128)(2,1)S(1)}, bf16[384,3072]{1,0:T(8,128)(2,1)}, u32[]{:S(2)}, u32[]{:S(2)}) collective-permute-start(bf16[384,3072]{1,0:T(8,128)(2,1)S(1)} %constant_dynamic-slice_fusion), channel_id=1, source_target_pairs={{3,2},{7,6},{11,10},{15,14},{19,18},{23,22},{27,26},{31,30}} | collective-permute-start | bytes 7077896 | tf_op jit(solution)/shard_map/ppermute | solution.py:130
  31.0 38.1 %collective-permute-start.3 = (bf16[384,2048]{1,0:T(8,128)(2,1)}, bf16[384,2048]{1,0:T(8,128)(2,1)}, u32[]{:S(2)}, u32[]{:S(2)}) collective-permute-start(bf16[384,2048]{1,0:T(8,128)(2,1)} %bitcast.6), channel_id=1, source_target_pairs={{1,0},{2,1},{3,2},{5,4},{6,5},{7,6},{9,8},{10,9},{11,10},{13,12},{... | collective-permute-start | bytes 4718600 | tf_op jit(solution)/shard_map/ppermute | solution.py:130
  32.3 79.5 %collective-permute-start.4 = (bf16[384,2048]{1,0:T(8,128)(2,1)}, bf16[384,2048]{1,0:T(8,128)(2,1)}, u32[]{:S(2)}, u32[]{:S(2)}) collective-permute-start(bf16[384,2048]{1,0:T(8,128)(2,1)} %bitcast.6), channel_id=1, source_target_pairs={{0,1},{1,2},{2,3},{4,5},{5,6},{6,7},{8,9},{9,10},{10,11},{12,13},{... | collective-permute-start | bytes 4718600 | tf_op jit(solution)/shard_map/ppermute | solution.py:126
  69.1 85.7 %collective-permute-start.8 = (bf16[384,2048]{1,0:T(8,128)(2,1)}, bf16[384,2048]{1,0:T(8,128)(2,1)}, u32[]{:S(2)}, u32[]{:S(2)}) collective-permute-start(bf16[384,2048]{1,0:T(8,128)(2,1)} %collective-permute-done.3), channel_id=1, source_target_pairs={{1,0},{2,1},{5,4},{6,5},{9,8},{10,9},{13,12},{14,13},{17,16},{18,1... | collective-permute-start | bytes 4718600 | tf_op jit(solution)/shard_map/ppermute | solution.py:130
  111.8 44.3 %collective-permute-start.9 = (bf16[384,2048]{1,0:T(8,128)(2,1)}, bf16[384,2048]{1,0:T(8,128)(2,1)}, u32[]{:S(2)}, u32[]{:S(2)}) collective-permute-start(bf16[384,2048]{1,0:T(8,128)(2,1)} %collective-permute-done.4), channel_id=1, source_target_pairs={{1,2},{2,3},{5,6},{6,7},{9,10},{10,11},{13,14},{14,15},{17,18},{18... | collective-permute-start | bytes 4718600 | tf_op jit(solution)/shard_map/ppermute | solution.py:126
  121.7 61.4 %collective-permute-start.32 = (bf16[384,3072]{1,0:T(8,128)(2,1)}, bf16[384,3072]{1,0:T(8,128)(2,1)S(1)}, u32[]{:S(2)}, u32[]{:S(2)}) collective-permute-start(bf16[384,3072]{1,0:T(8,128)(2,1)} %get-tuple-element.11), channel_id=1, source_target_pairs={{0,1},{1,2},{4,5},{5,6},{8,9},{9,10},{12,13},{13,14},{16,17},{17,1... | collective-permute-start | bytes 7077896 | tf_op jit(solution)/shard_map/ppermute | solution.py:126
  133.6 49.5 %collective-permute-start.35 = (bf16[384,3072]{1,0:T(8,128)(2,1)}, bf16[384,3072]{1,0:T(8,128)(2,1)}, u32[]{:S(2)}, u32[]{:S(2)}) collective-permute-start(bf16[384,3072]{1,0:T(8,128)(2,1)} %get-tuple-element.12), channel_id=1, source_target_pairs={{2,1},{3,2},{6,5},{7,6},{10,9},{11,10},{14,13},{15,14},{18,17},{19... | collective-permute-start | bytes 7077896 | tf_op jit(solution)/shard_map/ppermute | solution.py:130
  154.8 60.3 %collective-permute-start.13 = (bf16[384,2048]{1,0:T(8,128)(2,1)}, bf16[384,2048]{1,0:T(8,128)(2,1)}, u32[]{:S(2)}, u32[]{:S(2)}) collective-permute-start(bf16[384,2048]{1,0:T(8,128)(2,1)} %collective-permute-done.8), channel_id=1, source_target_pairs={{1,0},{5,4},{9,8},{13,12},{17,16},{21,20},{25,24},{29,28}} | collective-permute-start | bytes 4718600 | tf_op jit(solution)/shard_map/ppermute | solution.py:130
  156.1 59.0 %collective-permute-start.14 = (bf16[384,2048]{1,0:T(8,128)(2,1)}, bf16[384,2048]{1,0:T(8,128)(2,1)}, u32[]{:S(2)}, u32[]{:S(2)}) collective-permute-start(bf16[384,2048]{1,0:T(8,128)(2,1)} %collective-permute-done.9), channel_id=1, source_target_pairs={{2,3},{6,7},{10,11},{14,15},{18,19},{22,23},{26,27},{30,31}} | collective-permute-start | bytes 4718600 | tf_op jit(solution)/shard_map/ppermute | solution.py:126
  188.4 94.4 %collective-permute-start.33 = (bf16[384,3072]{1,0:T(8,128)(2,1)S(1)}, bf16[384,3072]{1,0:T(8,128)(2,1)S(1)}, u32[]{:S(2)}, u32[]{:S(2)}) collective-permute-start(bf16[384,3072]{1,0:T(8,128)(2,1)S(1)} %get-tuple-element.13), channel_id=1, source_target_pairs={{0,1},{1,2},{2,3},{4,5},{5,6},{6,7},{8,9},{9,10},{10,11},{12,13},{... | collective-permute-start | bytes 7077896 | tf_op jit(solution)/shard_map/ppermute | solution.py:126
  213.6 69.2 %collective-permute-start.36 = (bf16[384,3072]{1,0:T(8,128)(2,1)S(1)}, bf16[384,3072]{1,0:T(8,128)(2,1)S(1)}, u32[]{:S(2)}, u32[]{:S(2)}) collective-permute-start(bf16[384,3072]{1,0:T(8,128)(2,1)S(1)} %get-tuple-element.14), channel_id=1, source_target_pairs={{1,0},{2,1},{3,2},{5,4},{6,5},{7,6},{9,8},{10,9},{11,10},{13,12},{... | collective-permute-start | bytes 7077896 | tf_op jit(solution)/shard_map/ppermute | solution.py:130
  224.6 17.7 %collective-permute-start.6 = (bf16[384,512]{1,0:T(8,128)(2,1)S(1)}, bf16[384,512]{1,0:T(8,128)(2,1)S(1)}, u32[]{:S(2)}, u32[]{:S(2)}) collective-permute-start(bf16[384,512]{1,0:T(8,128)(2,1)S(1)} %get-tuple-element.33), channel_id=1, source_target_pairs={{0,8},{4,12},{8,0},{12,4},{1,9},{5,13},{9,1},{13,5},{2,10},{6,14},... | collective-permute-start | bytes 1179656 | tf_op jit(solution)/shard_map/ppermute | solution.py:119
  226.1 19.1 %collective-permute-start.7 = (bf16[384,512]{1,0:T(8,128)(2,1)S(1)}, bf16[384,512]{1,0:T(8,128)(2,1)S(1)}, u32[]{:S(2)}, u32[]{:S(2)}) collective-permute-start(bf16[384,512]{1,0:T(8,128)(2,1)S(1)} %get-tuple-element.32), channel_id=1, source_target_pairs={{0,12},{4,8},{8,4},{12,0},{1,13},{5,9},{9,5},{13,1},{2,14},{6,10},... | collective-permute-start | bytes 1179656 | tf_op jit(solution)/shard_map/ppermute | solution.py:119
  235.2 16.9 %collective-permute-start.10 = (bf16[384,512]{1,0:T(8,128)(2,1)S(1)}, bf16[384,512]{1,0:T(8,128)(2,1)S(1)}, u32[]{:S(2)}, u32[]{:S(2)}) collective-permute-start(bf16[384,512]{1,0:T(8,128)(2,1)S(1)} %get-tuple-element.28), channel_id=1, source_target_pairs={{0,4},{4,0},{8,12},{12,8},{1,5},{5,1},{9,13},{13,9},{2,6},{6,2},{1... | collective-permute-start | bytes 1179656 | tf_op jit(solution)/shard_map/ppermute | solution.py:119
  242.3 19.7 %collective-permute-start.11 = (bf16[384,512]{1,0:T(8,128)(2,1)S(1)}, bf16[384,512]{1,0:T(8,128)(2,1)S(1)}, u32[]{:S(2)}, u32[]{:S(2)}) collective-permute-start(bf16[384,512]{1,0:T(8,128)(2,1)S(1)} %get-tuple-element.30), channel_id=1, source_target_pairs={{0,8},{4,12},{8,0},{12,4},{1,9},{5,13},{9,1},{13,5},{2,10},{6,14},... | collective-permute-start | bytes 1179656 | tf_op jit(solution)/shard_map/ppermute | solution.py:119
  245.2 18.4 %collective-permute-start.12 = (bf16[384,512]{1,0:T(8,128)(2,1)S(1)}, bf16[384,512]{1,0:T(8,128)(2,1)S(1)}, u32[]{:S(2)}, u32[]{:S(2)}) collective-permute-start(bf16[384,512]{1,0:T(8,128)(2,1)S(1)} %get-tuple-element.29), channel_id=1, source_target_pairs={{0,12},{4,8},{8,4},{12,0},{1,13},{5,9},{9,5},{13,1},{2,14},{6,10},... | collective-permute-start | bytes 1179656 | tf_op jit(solution)/shard_map/ppermute | solution.py:119
  252.1 16.9 %collective-permute-start.15 = (bf16[384,512]{1,0:T(8,128)(2,1)S(1)}, bf16[384,512]{1,0:T(8,128)(2,1)S(1)}, u32[]{:S(2)}, u32[]{:S(2)}) collective-permute-start(bf16[384,512]{1,0:T(8,128)(2,1)S(1)} %get-tuple-element.22), channel_id=1, source_target_pairs={{0,4},{4,0},{8,12},{12,8},{1,5},{5,1},{9,13},{13,9},{2,6},{6,2},{1... | collective-permute-start | bytes 1179656 | tf_op jit(solution)/shard_map/ppermute | solution.py:119
  262.0 15.1 %collective-permute-start.16 = (bf16[384,512]{1,0:T(8,128)(2,1)S(1)}, bf16[384,512]{1,0:T(8,128)(2,1)S(1)}, u32[]{:S(2)}, u32[]{:S(2)}) collective-permute-start(bf16[384,512]{1,0:T(8,128)(2,1)S(1)} %get-tuple-element.24), channel_id=1, source_target_pairs={{0,8},{4,12},{8,0},{12,4},{1,9},{5,13},{9,1},{13,5},{2,10},{6,14},... | collective-permute-start | bytes 1179656 | tf_op jit(solution)/shard_map/ppermute | solution.py:119
  263.5 13.6 %collective-permute-start.17 = (bf16[384,512]{1,0:T(8,128)(2,1)S(1)}, bf16[384,512]{1,0:T(8,128)(2,1)S(1)}, u32[]{:S(2)}, u32[]{:S(2)}) collective-permute-start(bf16[384,512]{1,0:T(8,128)(2,1)S(1)} %get-tuple-element.23), channel_id=1, source_target_pairs={{0,12},{4,8},{8,4},{12,0},{1,13},{5,9},{9,5},{13,1},{2,14},{6,10},... | collective-permute-start | bytes 1179656 | tf_op jit(solution)/shard_map/ppermute | solution.py:119
  279.6 29.1 %collective-permute-start.18 = (bf16[384,1536]{1,0:T(8,128)(2,1)}, bf16[384,1536]{1,0:T(8,128)(2,1)S(1)}, u32[]{:S(2)}, u32[]{:S(2)}) collective-permute-start(bf16[384,1536]{1,0:T(8,128)(2,1)} %convolution_convert_fusion.3), channel_id=1, source_target_pairs={{0,4},{4,0},{8,12},{12,8},{1,5},{5,1},{9,13},{13,9},{2,6},{6,2},{1... | collective-permute-start | bytes 3538952 | tf_op jit(solution)/shard_map/ppermute | solution.py:119
  281.5 49.5 %collective-permute-start.19 = (bf16[384,1536]{1,0:T(8,128)(2,1)}, bf16[384,1536]{1,0:T(8,128)(2,1)}, u32[]{:S(2)}, u32[]{:S(2)}) collective-permute-start(bf16[384,1536]{1,0:T(8,128)(2,1)} %convolution_convert_fusion.2), channel_id=1, source_target_pairs={{0,8},{4,12},{8,0},{12,4},{1,9},{5,13},{9,1},{13,5},{2,10},{6,14},... | collective-permute-start | bytes 3538952 | tf_op jit(solution)/shard_map/ppermute | solution.py:119
  290.4 148.5 %collective-permute-start.43 = (bf16[1536,1536]{1,0:T(8,128)(2,1)}, bf16[1536,1536]{1,0:T(8,128)(2,1)}, u32[]{:S(2)}, u32[]{:S(2)}) collective-permute-start(bf16[1536,1536]{1,0:T(8,128)(2,1)} %convolution_convert_fusion), channel_id=1, source_target_pairs={{0,16},{16,0},{1,17},{17,1},{2,18},{18,2},{3,19},{19,3},{4,20},{20... | collective-permute-start | bytes 14155784 | tf_op jit(solution)/shard_map/ppermute | solution.py:119
  292.3 38.7 %collective-permute-start.20 = (bf16[384,1536]{1,0:T(8,128)(2,1)}, bf16[384,1536]{1,0:T(8,128)(2,1)}, u32[]{:S(2)}, u32[]{:S(2)}) collective-permute-start(bf16[384,1536]{1,0:T(8,128)(2,1)} %convolution_convert_fusion.1), channel_id=1, source_target_pairs={{0,12},{4,8},{8,4},{12,0},{1,13},{5,9},{9,5},{13,1},{2,14},{6,10},... | collective-permute-start | bytes 3538952 | tf_op jit(solution)/shard_map/ppermute | solution.py:119
  294.5 140.9 %collective-permute-start.37 = (bf16[384,3072]{1,0:T(8,128)(2,1)S(1)}, bf16[384,3072]{1,0:T(8,128)(2,1)}, u32[]{:S(2)}, u32[]{:S(2)}) collective-permute-start(bf16[384,3072]{1,0:T(8,128)(2,1)S(1)} %add_add_fusion.s3), channel_id=1, source_target_pairs={{1,0},{2,1},{3,2},{5,4},{6,5},{7,6},{9,8},{10,9},{11,10},{13,12},{... | collective-permute-start | bytes 7077896 | tf_op jit(solution)/shard_map/ppermute | solution.py:130
  336.5 26.6 %collective-permute-start.21 = (bf16[96,1536]{1,0:T(8,128)(2,1)}, bf16[96,1536]{1,0:T(8,128)(2,1)S(1)}, u32[]{:S(2)}, u32[]{:S(2)}) collective-permute-start(bf16[96,1536]{1,0:T(8,128)(2,1)} %get-tuple-element.40), channel_id=1, source_target_pairs={{0,1},{1,0},{2,3},{3,2},{4,5},{5,4},{6,7},{7,6},{8,9},{9,8},{10,11... | collective-permute-start | bytes 884744 | tf_op jit(solution)/shard_map/ppermute | solution.py:119
  338.9 27.2 %collective-permute-start.22 = (bf16[96,1536]{1,0:T(8,128)(2,1)S(1)}, bf16[96,1536]{1,0:T(8,128)(2,1)S(1)}, u32[]{:S(2)}, u32[]{:S(2)}) collective-permute-start(bf16[96,1536]{1,0:T(8,128)(2,1)S(1)} %get-tuple-element.42), channel_id=1, source_target_pairs={{0,2},{1,3},{2,0},{3,1},{4,6},{5,7},{6,4},{7,5},{8,10},{9,11},{10,... | collective-permute-start | bytes 884744 | tf_op jit(solution)/shard_map/ppermute | solution.py:119
  340.5 30.9 %collective-permute-start.23 = (bf16[96,1536]{1,0:T(8,128)(2,1)S(1)}, bf16[96,1536]{1,0:T(8,128)(2,1)}, u32[]{:S(2)}, u32[]{:S(2)}) collective-permute-start(bf16[96,1536]{1,0:T(8,128)(2,1)S(1)} %get-tuple-element.41), channel_id=1, source_target_pairs={{0,3},{1,2},{2,1},{3,0},{4,7},{5,6},{6,5},{7,4},{8,11},{9,10},{10,... | collective-permute-start | bytes 884744 | tf_op jit(solution)/shard_map/ppermute | solution.py:119
  363.0 74.5 %collective-permute-start.40 = (bf16[384,3072]{1,0:T(8,128)(2,1)S(1)}, bf16[384,3072]{1,0:T(8,128)(2,1)}, u32[]{:S(2)}, u32[]{:S(2)}) collective-permute-start(bf16[384,3072]{1,0:T(8,128)(2,1)S(1)} %add_add_fusion.s3), channel_id=1, source_target_pairs={{0,1},{1,2},{2,3},{4,5},{5,6},{6,7},{8,9},{9,10},{10,11},{12,13},{... | collective-permute-start | bytes 7077896 | tf_op jit(solution)/shard_map/ppermute | solution.py:126
  373.0 49.6 %collective-permute-start.24 = (bf16[96,1536]{1,0:T(8,128)(2,1)S(1)}, bf16[96,1536]{1,0:T(8,128)(2,1)S(1)}, u32[]{:S(2)}, u32[]{:S(2)}) collective-permute-start(bf16[96,1536]{1,0:T(8,128)(2,1)S(1)} %get-tuple-element.10), channel_id=1, source_target_pairs={{0,1},{1,0},{2,3},{3,2},{4,5},{5,4},{6,7},{7,6},{8,9},{9,8},{10,11... | collective-permute-start | bytes 884744 | tf_op jit(solution)/shard_map/ppermute | solution.py:119
  379.2 49.7 %collective-permute-start.25 = (bf16[96,1536]{1,0:T(8,128)(2,1)S(1)}, bf16[96,1536]{1,0:T(8,128)(2,1)S(1)}, u32[]{:S(2)}, u32[]{:S(2)}) collective-permute-start(bf16[96,1536]{1,0:T(8,128)(2,1)S(1)} %get-tuple-element.10), channel_id=1, source_target_pairs={{0,2},{1,3},{2,0},{3,1},{4,6},{5,7},{6,4},{7,5},{8,10},{9,11},{10,... | collective-permute-start | bytes 884744 | tf_op jit(solution)/shard_map/ppermute | solution.py:119
  434.0 29.1 %collective-permute-start.27 = (bf16[384,1536]{1,0:T(8,128)(2,1)S(1)}, bf16[384,1536]{1,0:T(8,128)(2,1)}, u32[]{:S(2)}, u32[]{:S(2)}) collective-permute-start(bf16[384,1536]{1,0:T(8,128)(2,1)S(1)} %constant_dynamic-update-slice_fusion.27), channel_id=1, source_target_pairs={{0,4},{4,0},{8,12},{12,8},{1,5},{5,1},{9,13},{13,9},{2,6},{6,2},{1... | collective-permute-start | bytes 3538952 | tf_op jit(solution)/shard_map/ppermute | solution.py:119
  434.1 32.2 %collective-permute-start.28 = (bf16[384,1536]{1,0:T(8,128)(2,1)S(1)}, bf16[384,1536]{1,0:T(8,128)(2,1)}, u32[]{:S(2)}, u32[]{:S(2)}) collective-permute-start(bf16[384,1536]{1,0:T(8,128)(2,1)S(1)} %constant_dynamic-update-slice_fusion.27), channel_id=1, source_target_pairs={{0,8},{4,12},{8,0},{12,4},{1,9},{5,13},{9,1},{13,5},{2,10},{6,14},... | collective-permute-start | bytes 3538952 | tf_op jit(solution)/shard_map/ppermute | solution.py:119
  435.4 53.5 %collective-permute-start.29 = (bf16[384,1536]{1,0:T(8,128)(2,1)S(1)}, bf16[384,1536]{1,0:T(8,128)(2,1)}, u32[]{:S(2)}, u32[]{:S(2)}) collective-permute-start(bf16[384,1536]{1,0:T(8,128)(2,1)S(1)} %constant_dynamic-update-slice_fusion.27), channel_id=1, source_target_pairs={{0,12},{4,8},{8,4},{12,0},{1,13},{5,9},{9,5},{13,1},{2,14},{6,10},... | collective-permute-start | bytes 3538952 | tf_op jit(solution)/shard_map/ppermute | solution.py:119
  437.6 112.6 %collective-permute-start.38 = (bf16[384,3072]{1,0:T(8,128)(2,1)}, bf16[384,3072]{1,0:T(8,128)(2,1)}, u32[]{:S(2)}, u32[]{:S(2)}) collective-permute-start(bf16[384,3072]{1,0:T(8,128)(2,1)} %collective-permute-done.37), channel_id=1, source_target_pairs={{1,0},{2,1},{5,4},{6,5},{9,8},{10,9},{13,12},{14,13},{17,16},{18,1... | collective-permute-start | bytes 7077896 | tf_op jit(solution)/shard_map/ppermute | solution.py:130
  438.9 112.6 %collective-permute-start.41 = (bf16[384,3072]{1,0:T(8,128)(2,1)}, bf16[384,3072]{1,0:T(8,128)(2,1)}, u32[]{:S(2)}, u32[]{:S(2)}) collective-permute-start(bf16[384,3072]{1,0:T(8,128)(2,1)} %collective-permute-done.40), channel_id=1, source_target_pairs={{1,2},{2,3},{5,6},{6,7},{9,10},{10,11},{13,14},{14,15},{17,18},{18... | collective-permute-start | bytes 7077896 | tf_op jit(solution)/shard_map/ppermute | solution.py:126
  463.1 50.6 %collective-permute-start.44 = (bf16[384,1536]{1,0:T(8,128)(2,1)S(1)}, bf16[384,1536]{1,0:T(8,128)(2,1)}, u32[]{:S(2)}, u32[]{:S(2)}) collective-permute-start(bf16[384,1536]{1,0:T(8,128)(2,1)S(1)} %fusion.36), channel_id=1, source_target_pairs={{0,4},{4,0},{8,12},{12,8},{1,5},{5,1},{9,13},{13,9},{2,6},{6,2},{1... | collective-permute-start | bytes 3538952 | tf_op jit(solution)/shard_map/ppermute | solution.py:119
  466.3 47.8 %collective-permute-start.45 = (bf16[384,1536]{1,0:T(8,128)(2,1)}, bf16[384,1536]{1,0:T(8,128)(2,1)}, u32[]{:S(2)}, u32[]{:S(2)}) collective-permute-start(bf16[384,1536]{1,0:T(8,128)(2,1)} %fusion.37), channel_id=1, source_target_pairs={{0,8},{4,12},{8,0},{12,4},{1,9},{5,13},{9,1},{13,5},{2,10},{6,14},... | collective-permute-start | bytes 3538952 | tf_op jit(solution)/shard_map/ppermute | solution.py:119
  488.9 48.4 %collective-permute-start.46 = (bf16[384,1536]{1,0:T(8,128)(2,1)}, bf16[384,1536]{1,0:T(8,128)(2,1)}, u32[]{:S(2)}, u32[]{:S(2)}) collective-permute-start(bf16[384,1536]{1,0:T(8,128)(2,1)} %fusion.38), channel_id=1, source_target_pairs={{0,12},{4,8},{8,4},{12,0},{1,13},{5,9},{9,5},{13,1},{2,14},{6,10},... | collective-permute-start | bytes 3538952 | tf_op jit(solution)/shard_map/ppermute | solution.py:119
  513.7 139.3 %collective-permute-start.30 = (bf16[1536,1536]{1,0:T(8,128)(2,1)}, bf16[1536,1536]{1,0:T(8,128)(2,1)}, u32[]{:S(2)}, u32[]{:S(2)}) collective-permute-start(bf16[1536,1536]{1,0:T(8,128)(2,1)} %constant_dynamic-update-slice_fusion.23.mine_ref), channel_id=1, source_target_pairs={{0,16},{16,0},{1,17},{17,1},{2,18},{18,2},{3,19},{19,3},{4,20},{20... | collective-permute-start | bytes 14155784 | tf_op jit(solution)/shard_map/ppermute | solution.py:119
  542.3 17.5 %collective-permute-start.47 = (bf16[96,1536]{1,0:T(8,128)(2,1)S(1)}, bf16[96,1536]{1,0:T(8,128)(2,1)S(1)}, u32[]{:S(2)}, u32[]{:S(2)}) collective-permute-start(bf16[96,1536]{1,0:T(8,128)(2,1)S(1)} %get-tuple-element.37), channel_id=1, source_target_pairs={{0,1},{1,0},{2,3},{3,2},{4,5},{5,4},{6,7},{7,6},{8,9},{9,8},{10,11... | collective-permute-start | bytes 884744 | tf_op jit(solution)/shard_map/ppermute | solution.py:119
  550.2 93.9 %collective-permute-start.39 = (bf16[384,3072]{1,0:T(8,128)(2,1)}, bf16[384,3072]{1,0:T(8,128)(2,1)}, u32[]{:S(2)}, u32[]{:S(2)}) collective-permute-start(bf16[384,3072]{1,0:T(8,128)(2,1)} %collective-permute-done.38), channel_id=1, source_target_pairs={{1,0},{5,4},{9,8},{13,12},{17,16},{21,20},{25,24},{29,28}} | collective-permute-start | bytes 7077896 | tf_op jit(solution)/shard_map/ppermute | solution.py:130
  551.5 94.5 %collective-permute-start.42 = (bf16[384,3072]{1,0:T(8,128)(2,1)}, bf16[384,3072]{1,0:T(8,128)(2,1)}, u32[]{:S(2)}, u32[]{:S(2)}) collective-permute-start(bf16[384,3072]{1,0:T(8,128)(2,1)} %collective-permute-done.41), channel_id=1, source_target_pairs={{2,3},{6,7},{10,11},{14,15},{18,19},{22,23},{26,27},{30,31}} | collective-permute-start | bytes 7077896 | tf_op jit(solution)/shard_map/ppermute | solution.py:126
  553.8 24.4 %collective-permute-start.48 = (bf16[96,1536]{1,0:T(8,128)(2,1)S(1)}, bf16[96,1536]{1,0:T(8,128)(2,1)S(1)}, u32[]{:S(2)}, u32[]{:S(2)}) collective-permute-start(bf16[96,1536]{1,0:T(8,128)(2,1)S(1)} %get-tuple-element.39), channel_id=1, source_target_pairs={{0,2},{1,3},{2,0},{3,1},{4,6},{5,7},{6,4},{7,5},{8,10},{9,11},{10,... | collective-permute-start | bytes 884744 | tf_op jit(solution)/shard_map/ppermute | solution.py:119
  559.8 18.4 %collective-permute-start.49 = (bf16[96,1536]{1,0:T(8,128)(2,1)S(1)}, bf16[96,1536]{1,0:T(8,128)(2,1)S(1)}, u32[]{:S(2)}, u32[]{:S(2)}) collective-permute-start(bf16[96,1536]{1,0:T(8,128)(2,1)S(1)} %get-tuple-element.38), channel_id=1, source_target_pairs={{0,3},{1,2},{2,1},{3,0},{4,7},{5,6},{6,5},{7,4},{8,11},{9,10},{10,... | collective-permute-start | bytes 884744 | tf_op jit(solution)/shard_map/ppermute | solution.py:119
  579.5 52.3 %collective-permute-start.50 = (bf16[96,1536]{1,0:T(8,128)(2,1)S(1)}, bf16[96,1536]{1,0:T(8,128)(2,1)S(1)}, u32[]{:S(2)}, u32[]{:S(2)}) collective-permute-start(bf16[96,1536]{1,0:T(8,128)(2,1)S(1)} %get-tuple-element.6), channel_id=1, source_target_pairs={{0,1},{1,0},{2,3},{3,2},{4,5},{5,4},{6,7},{7,6},{8,9},{9,8},{10,11... | collective-permute-start | bytes 884744 | tf_op jit(solution)/shard_map/ppermute | solution.py:119
  586.4 48.8 %collective-permute-start.51 = (bf16[96,1536]{1,0:T(8,128)(2,1)S(1)}, bf16[96,1536]{1,0:T(8,128)(2,1)S(1)}, u32[]{:S(2)}, u32[]{:S(2)}) collective-permute-start(bf16[96,1536]{1,0:T(8,128)(2,1)S(1)} %get-tuple-element.6), channel_id=1, source_target_pairs={{0,2},{1,3},{2,0},{3,1},{4,6},{5,7},{6,4},{7,5},{8,10},{9,11},{10,... | collective-permute-start | bytes 884744 | tf_op jit(solution)/shard_map/ppermute | solution.py:119
  642.0 55.9 %collective-permute-start.53 = (bf16[384,1536]{1,0:T(8,128)(2,1)S(1)}, bf16[384,1536]{1,0:T(8,128)(2,1)S(1)}, u32[]{:S(2)}, u32[]{:S(2)}) collective-permute-start(bf16[384,1536]{1,0:T(8,128)(2,1)S(1)} %constant_dynamic-update-slice_fusion.16), channel_id=1, source_target_pairs={{0,4},{4,0},{8,12},{12,8},{1,5},{5,1},{9,13},{13,9},{2,6},{6,2},{1... | collective-permute-start | bytes 3538952 | tf_op jit(solution)/shard_map/ppermute | solution.py:119
  642.4 55.6 %collective-permute-start.54 = (bf16[384,1536]{1,0:T(8,128)(2,1)S(1)}, bf16[384,1536]{1,0:T(8,128)(2,1)S(1)}, u32[]{:S(2)}, u32[]{:S(2)}) collective-permute-start(bf16[384,1536]{1,0:T(8,128)(2,1)S(1)} %constant_dynamic-update-slice_fusion.16), channel_id=1, source_target_pairs={{0,8},{4,12},{8,0},{12,4},{1,9},{5,13},{9,1},{13,5},{2,10},{6,14},... | collective-permute-start | bytes 3538952 | tf_op jit(solution)/shard_map/ppermute | solution.py:119
  644.1 54.0 %collective-permute-start.55 = (bf16[384,1536]{1,0:T(8,128)(2,1)S(1)}, bf16[384,1536]{1,0:T(8,128)(2,1)S(1)}, u32[]{:S(2)}, u32[]{:S(2)}) collective-permute-start(bf16[384,1536]{1,0:T(8,128)(2,1)S(1)} %constant_dynamic-update-slice_fusion.16), channel_id=1, source_target_pairs={{0,12},{4,8},{8,4},{12,0},{1,13},{5,9},{9,5},{13,1},{2,14},{6,10},... | collective-permute-start | bytes 3538952 | tf_op jit(solution)/shard_map/ppermute | solution.py:119
  700.7 20.3 %collective-permute-start.57 = (bf16[384,512]{1,0:T(8,128)(2,1)S(1)}, bf16[384,512]{1,0:T(8,128)(2,1)S(1)}, u32[]{:S(2)}, u32[]{:S(2)}) collective-permute-start(bf16[384,512]{1,0:T(8,128)(2,1)S(1)} %get-tuple-element.52), channel_id=1, source_target_pairs={{0,8},{4,12},{8,0},{12,4},{1,9},{5,13},{9,1},{13,5},{2,10},{6,14},... | collective-permute-start | bytes 1179656 | tf_op jit(solution)/shard_map/ppermute | solution.py:119
  702.0 19.3 %collective-permute-start.58 = (bf16[384,512]{1,0:T(8,128)(2,1)S(1)}, bf16[384,512]{1,0:T(8,128)(2,1)S(1)}, u32[]{:S(2)}, u32[]{:S(2)}) collective-permute-start(bf16[384,512]{1,0:T(8,128)(2,1)S(1)} %get-tuple-element.52), channel_id=1, source_target_pairs={{0,12},{4,8},{8,4},{12,0},{1,13},{5,9},{9,5},{13,1},{2,14},{6,10},... | collective-permute-start | bytes 1179656 | tf_op jit(solution)/shard_map/ppermute | solution.py:119
  704.8 29.9 %collective-permute-start.59 = (bf16[384,512]{1,0:T(8,128)(2,1)S(1)}, bf16[384,512]{1,0:T(8,128)(2,1)S(1)}, u32[]{:S(2)}, u32[]{:S(2)}) collective-permute-start(bf16[384,512]{1,0:T(8,128)(2,1)S(1)} %get-tuple-element.50), channel_id=1, source_target_pairs={{0,4},{4,0},{8,12},{12,8},{1,5},{5,1},{9,13},{13,9},{2,6},{6,2},{1... | collective-permute-start | bytes 1179656 | tf_op jit(solution)/shard_map/ppermute | solution.py:119
  705.2 31.2 %collective-permute-start.60 = (bf16[384,512]{1,0:T(8,128)(2,1)S(1)}, bf16[384,512]{1,0:T(8,128)(2,1)S(1)}, u32[]{:S(2)}, u32[]{:S(2)}) collective-permute-start(bf16[384,512]{1,0:T(8,128)(2,1)S(1)} %get-tuple-element.50), channel_id=1, source_target_pairs={{0,8},{4,12},{8,0},{12,4},{1,9},{5,13},{9,1},{13,5},{2,10},{6,14},... | collective-permute-start | bytes 1179656 | tf_op jit(solution)/shard_map/ppermute | solution.py:119
  712.4 25.8 %collective-permute-start.61 = (bf16[384,512]{1,0:T(8,128)(2,1)S(1)}, bf16[384,512]{1,0:T(8,128)(2,1)S(1)}, u32[]{:S(2)}, u32[]{:S(2)}) collective-permute-start(bf16[384,512]{1,0:T(8,128)(2,1)S(1)} %get-tuple-element.50), channel_id=1, source_target_pairs={{0,12},{4,8},{8,4},{12,0},{1,13},{5,9},{9,5},{13,1},{2,14},{6,10},... | collective-permute-start | bytes 1179656 | tf_op jit(solution)/shard_map/ppermute | solution.py:119
  729.3 30.8 %collective-permute-start.68 = (bf16[384,2048]{1,0:T(8,128)(2,1)S(1)}, bf16[384,2048]{1,0:T(8,128)(2,1)S(1)}, u32[]{:S(2)}, u32[]{:S(2)}) collective-permute-start(bf16[384,2048]{1,0:T(8,128)(2,1)S(1)} %fusion.48), channel_id=1, source_target_pairs={{0,1},{4,5},{8,9},{12,13},{16,17},{20,21},{24,25},{28,29}} | collective-permute-start | bytes 4718600 | tf_op jit(solution)/shard_map/ppermute | solution.py:126
  732.7 27.4 %collective-permute-start.71 = (bf16[384,2048]{1,0:T(8,128)(2,1)S(1)}, bf16[384,2048]{1,0:T(8,128)(2,1)S(1)}, u32[]{:S(2)}, u32[]{:S(2)}) collective-permute-start(bf16[384,2048]{1,0:T(8,128)(2,1)S(1)} %fusion.48), channel_id=1, source_target_pairs={{3,2},{7,6},{11,10},{15,14},{19,18},{23,22},{27,26},{31,30}} | collective-permute-start | bytes 4718600 | tf_op jit(solution)/shard_map/ppermute | solution.py:130
  734.7 28.3 %collective-permute-start.62 = (bf16[384,512]{1,0:T(8,128)(2,1)S(1)}, bf16[384,512]{1,0:T(8,128)(2,1)S(1)}, u32[]{:S(2)}, u32[]{:S(2)}) collective-permute-start(bf16[384,512]{1,0:T(8,128)(2,1)S(1)} %get-tuple-element.48), channel_id=1, source_target_pairs={{0,4},{4,0},{8,12},{12,8},{1,5},{5,1},{9,13},{13,9},{2,6},{6,2},{1... | collective-permute-start | bytes 1179656 | tf_op jit(solution)/shard_map/ppermute | solution.py:119
  736.4 31.0 %collective-permute-start.63 = (bf16[384,512]{1,0:T(8,128)(2,1)S(1)}, bf16[384,512]{1,0:T(8,128)(2,1)S(1)}, u32[]{:S(2)}, u32[]{:S(2)}) collective-permute-start(bf16[384,512]{1,0:T(8,128)(2,1)S(1)} %get-tuple-element.48), channel_id=1, source_target_pairs={{0,8},{4,12},{8,0},{12,4},{1,9},{5,13},{9,1},{13,5},{2,10},{6,14},... | collective-permute-start | bytes 1179656 | tf_op jit(solution)/shard_map/ppermute | solution.py:119
  738.2 30.1 %collective-permute-start.64 = (bf16[384,512]{1,0:T(8,128)(2,1)S(1)}, bf16[384,512]{1,0:T(8,128)(2,1)S(1)}, u32[]{:S(2)}, u32[]{:S(2)}) collective-permute-start(bf16[384,512]{1,0:T(8,128)(2,1)S(1)} %get-tuple-element.48), channel_id=1, source_target_pairs={{0,12},{4,8},{8,4},{12,0},{1,13},{5,9},{9,5},{13,1},{2,14},{6,10},... | collective-permute-start | bytes 1179656 | tf_op jit(solution)/shard_map/ppermute | solution.py:119
  763.0 32.8 %collective-permute-start.69 = (bf16[384,2048]{1,0:T(8,128)(2,1)S(1)}, bf16[384,2048]{1,0:T(8,128)(2,1)S(1)}, u32[]{:S(2)}, u32[]{:S(2)}) collective-permute-start(bf16[384,2048]{1,0:T(8,128)(2,1)S(1)} %get-tuple-element.20), channel_id=1, source_target_pairs={{0,1},{1,2},{4,5},{5,6},{8,9},{9,10},{12,13},{13,14},{16,17},{17,1... | collective-permute-start | bytes 4718600 | tf_op jit(solution)/shard_map/ppermute | solution.py:126
  767.5 28.3 %collective-permute-start.72 = (bf16[384,2048]{1,0:T(8,128)(2,1)S(1)}, bf16[384,2048]{1,0:T(8,128)(2,1)S(1)}, u32[]{:S(2)}, u32[]{:S(2)}) collective-permute-start(bf16[384,2048]{1,0:T(8,128)(2,1)S(1)} %get-tuple-element.21), channel_id=1, source_target_pairs={{2,1},{3,2},{6,5},{7,6},{10,9},{11,10},{14,13},{15,14},{18,17},{19... | collective-permute-start | bytes 4718600 | tf_op jit(solution)/shard_map/ppermute | solution.py:130
  797.2 36.6 %collective-permute-start.70 = (bf16[384,2048]{1,0:T(8,128)(2,1)S(1)}, bf16[384,2048]{1,0:T(8,128)(2,1)}, u32[]{:S(2)}, u32[]{:S(2)}) collective-permute-start(bf16[384,2048]{1,0:T(8,128)(2,1)S(1)} %get-tuple-element.18), channel_id=1, source_target_pairs={{0,1},{1,2},{2,3},{4,5},{5,6},{6,7},{8,9},{9,10},{10,11},{12,13},{... | collective-permute-start | bytes 4718600 | tf_op jit(solution)/shard_map/ppermute | solution.py:126
  803.1 30.7 %collective-permute-start.73 = (bf16[384,2048]{1,0:T(8,128)(2,1)S(1)}, bf16[384,2048]{1,0:T(8,128)(2,1)}, u32[]{:S(2)}, u32[]{:S(2)}) collective-permute-start(bf16[384,2048]{1,0:T(8,128)(2,1)S(1)} %get-tuple-element.19), channel_id=1, source_target_pairs={{1,0},{2,1},{3,2},{5,4},{6,5},{7,6},{9,8},{10,9},{11,10},{13,12},{... | collective-permute-start | bytes 4718600 | tf_op jit(solution)/shard_map/ppermute | solution.py:130
  (32 other events, 606.9 us)

commit v2 on v0

v2 whole, which is shorter than its diff:
```python
import functools

import jax
import jax.numpy as jnp
from jax import lax
from jax.experimental import pallas as pl
from jax.experimental.pallas import tpu as pltpu
from jax.sharding import PartitionSpec as P

BW = 128
F32 = jnp.float32
BF16 = jnp.bfloat16
I32 = jnp.int32
VMEM = 48 * 2**20


def mm(a, b, contract):
    return lax.dot_general(a, b, (contract, ((), ())), preferred_element_type=F32)


def take(x, start, size, axis):
    return lax.dynamic_slice_in_dim(x, start, size, axis)


def after(x, *others):
    return lax.optimization_barrier((x, *others))[0]


def swap(x, axis, d):
    n = lax.axis_size(axis)
    return lax.ppermute(x, axis, [(i, i ^ d) for i in range(n)])


def pick_kernel(band, place, spot, root_ref, *outs):
    for d, out in enumerate(outs):
        out[...] = root_ref[pl.ds(pl.multiple_of(spot[d] * band, band), band), :]


def pick(root, place, spot, parts):
    rows, count = root.shape[0], place.shape[0]
    band = rows // parts
    return pl.pallas_call(
        functools.partial(pick_kernel, band),
        grid_spec=pltpu.PrefetchScalarGridSpec(
            num_scalar_prefetch=2,
            grid=(count,),
            in_specs=[pl.BlockSpec((rows, BW), lambda k, place, spot: (0, place[k]))],
            out_specs=[pl.BlockSpec((band, BW), lambda k, place, spot: (0, k))] * parts,
        ),
        out_shape=[jax.ShapeDtypeStruct((band, count * BW), BF16)] * parts,
        cost_estimate=pl.CostEstimate(
            flops=0, bytes_accessed=4 * rows * count * BW, transcendentals=0
        ),
    )(place, spot, root)


def assemble_kernel(source, rank, *refs):
    pieces, out = refs[:-1], refs[-1]
    slots = out.shape[1] // BW
    for s in range(slots):
        for d, piece in enumerate(pieces):

            @pl.when(source[s] == d)
            def _():
                start = pl.multiple_of(rank[s] * BW, BW)
                out[:, s * BW : (s + 1) * BW] = piece[:, pl.ds(start, BW)]


def assemble(pieces, source, rank):
    band, slots = pieces[0].shape[0], source.shape[0]
    whole = lambda shape: pl.BlockSpec(shape, lambda i, source, rank: (0, 0))
    return pl.pallas_call(
        assemble_kernel,
        grid_spec=pltpu.PrefetchScalarGridSpec(
            num_scalar_prefetch=2,
            grid=(1,),
            in_specs=[whole(p.shape) for p in pieces],
            out_specs=whole((band, slots * BW)),
        ),
        out_shape=jax.ShapeDtypeStruct((band, slots * BW), BF16),
        compiler_params=pltpu.CompilerParams(vmem_limit_bytes=VMEM),
        cost_estimate=pl.CostEstimate(
            flops=0, bytes_accessed=6 * band * slots * BW, transcendentals=0
        ),
    )(source, rank, *pieces)


def unfold_kernel(count, half, packed_ref, out_ref):
    i = pl.program_id(0)
    for d in range(half + 1):
        j = lax.rem(i + d, count)
        out_ref[:, pl.ds(pl.multiple_of(j * BW, BW), BW)] = packed_ref[
            pl.ds(pl.multiple_of(i * BW, BW), BW), d * BW : (d + 1) * BW
        ]
    for d in range(1, count - half):
        j = lax.rem(i + count - d, count)
        block = packed_ref[pl.ds(pl.multiple_of(j * BW, BW), BW), d * BW : (d + 1) * BW]
        out_ref[:, pl.ds(pl.multiple_of(j * BW, BW), BW)] = block.T


def unfold(packed):
    width = packed.shape[0]
    count = width // BW
    return pl.pallas_call(
        functools.partial(unfold_kernel, count, count // 2),
        grid=(count,),
        in_specs=[pl.BlockSpec(packed.shape, lambda i: (0, 0))],
        out_specs=pl.BlockSpec((BW, width), lambda i: (i, 0)),
        out_shape=jax.ShapeDtypeStruct((width, width), BF16),
        compiler_params=pltpu.CompilerParams(vmem_limit_bytes=VMEM),
        cost_estimate=pl.CostEstimate(
            flops=0, bytes_accessed=4 * width * width, transcendentals=0
        ),
    )(packed)


def finish_kernel(block, at, has, root_ref, weight_ref, mine_ref, other_ref, all_ref, base, out_ref):
    k = pl.program_id(0)
    width = mine_ref.shape[0]

    @pl.when((k == 0) | (block[k] != block[lax.max(k - 1, 0)]))
    def _():
        out = 2.0 * root_ref[...].astype(F32) * weight_ref[...].astype(F32)
        for w, adjoint in enumerate((mine_ref, other_ref)):
            lifted = jnp.dot(
                all_ref[:, w * width : (w + 1) * width],
                adjoint[...],
                preferred_element_type=F32,
            )
            keep = jnp.where(has[w, k] == 1, 2.0, 0.0).astype(F32)
            out = out + keep * lifted.astype(BF16).astype(F32)
        out_ref[...] = out.astype(BF16)


def finish(base, root, weights, mine, other, selected, block, at, has):
    rows = root.shape[0]
    width = mine.shape[0]
    steps = block.shape[0]
    strip = pl.BlockSpec((rows, BW), lambda k, block, at, has: (0, block[k]))
    return pl.pallas_call(
        finish_kernel,
        grid_spec=pltpu.PrefetchScalarGridSpec(
            num_scalar_prefetch=3,
            grid=(steps,),
            in_specs=[
                strip,
                pl.BlockSpec((1, BW), lambda k, block, at, has: (0, block[k])),
                pl.BlockSpec((width, BW), lambda k, block, at, has: (0, at[0, k])),
                pl.BlockSpec((width, BW), lambda k, block, at, has: (0, at[1, k])),
                pl.BlockSpec(selected.shape, lambda k, block, at, has: (0, 0)),
                pl.BlockSpec(memory_space=pl.ANY),
            ],
            out_specs=strip,
        ),
        out_shape=jax.ShapeDtypeStruct(base.shape, BF16),
        input_output_aliases={8: 0},
        compiler_params=pltpu.CompilerParams(vmem_limit_bytes=VMEM),
        cost_estimate=pl.CostEstimate(
            flops=2 * rows * width * width,
            bytes_accessed=2 * rows * 4 * width,
            transcendentals=0,
        ),
    )(block, at, has, root, weights, mine, other, selected, base)


FAR, MIDDLE, NEAR = (3, 3, 0, 0), (2, 2, 1, 1), (1, 0, 3, 2)


def up(x, lo, hi):
    return lax.ppermute(x, "col", [(i, i + 1) for i in range(lo, hi + 1)])


def down(x, lo, hi):
    return lax.ppermute(x, "col", [(i, i - 1) for i in range(lo, hi + 1)])


def add(a, b):
    return (a.astype(F32) + b.astype(F32)).astype(BF16)


def line_scatter(chunks, z):
    far, middle, near, own = chunks
    up1, down1 = up(far, 0, 0), down(far, 3, 3)
    up2 = up(add(jnp.where(z == 0, middle, far), up1), 0, 1)
    down2 = down(add(jnp.where(z == 3, middle, far), down1), 2, 3)
    up3 = up(add(jnp.where(z == 1, middle, near), up2), 0, 2)
    down3 = down(add(jnp.where(z == 2, middle, near), down2), 1, 3)
    total = own.astype(F32) + up3.astype(F32) + down3.astype(F32)
    return total.astype(BF16)


def row_scatter(chunk, r, n):
    if n != 4:
        parts = jnp.stack([chunk(i).astype(BF16) for i in range(n)])
        return lax.psum_scatter(parts, "row", scatter_dimension=0, tiled=False).astype(F32)
    arrived = [swap(chunk(r ^ d).astype(BF16), "row", d) for d in (1, 2, 3)]
    return sum((a.astype(F32) for a in arrived), chunk(r).astype(F32))


def row_gather(x, r, n, axis):
    if n != 4:
        return lax.all_gather(x, "row", axis=axis, tiled=True)
    shape = list(x.shape)
    step = shape[axis]
    shape[axis] = step * n
    whole = jnp.zeros(shape, x.dtype)
    for d in range(n):
        piece = swap(x, "row", d) if d else x
        whole = lax.dynamic_update_slice_in_dim(whole, piece, (r ^ d) * step, axis)
    return whole


def col_scatter(x, z):
    n = lax.axis_size("col")
    step = x.shape[0] // n
    piece = lambda i: take(x, i * step, step, 0)
    arrived = [swap(piece(z ^ d).astype(BF16), "col", d) for d in range(1, n)]
    return sum((a.astype(F32) for a in arrived), piece(z)).astype(BF16)


def col_gather(x, z):
    n = lax.axis_size("col")
    step = x.shape[0]
    whole = jnp.zeros((step * n, *x.shape[1:]), x.dtype)
    for d in range(n):
        part = swap(x, "col", d) if d else x
        whole = lax.dynamic_update_slice_in_dim(whole, part, (z ^ d) * step, 0)
    return whole


def symmetric_rows(left, right, axis, strip):
    contract = ((1 - axis,), (1 - axis,))
    if strip % BW:
        return lambda i: mm(take(left, i * strip, strip, axis), right, contract)
    half = left.shape[axis] // BW // 2 + 1
    own = strip // BW
    reach = (own - 1 + half) * BW
    again = lax.slice_in_dim(right, 0, reach - strip, axis=axis)
    longer = jnp.concatenate([right, again], axis=axis)

    def rows(i):
        product = mm(
            take(left, i * strip, strip, axis), take(longer, i * strip, reach, axis), contract
        ).astype(BF16)
        bands = [
            product[b * BW : (b + 1) * BW, b * BW : (b + half) * BW] for b in range(own)
        ]
        return jnp.concatenate(bands, axis=0)

    return rows


def symmetric_whole(rows, strip, r, n):
    whole = row_gather(rows, r, n, 0)
    return whole if strip % BW else unfold(whole)


def program(capacity, root, child_inverse, coupling, child_weights, root_weights, owner, inside):
    g, r, z = lax.axis_index("grp"), lax.axis_index("row"), lax.axis_index("col")
    nrow, ncol = lax.axis_size("row"), lax.axis_size("col")
    root_cols = root.shape[1]
    blocks = root_cols // BW
    factor, links = child_inverse[0], coupling[0]
    weights = child_weights[0].astype(F32)
    share = links.shape[0]
    width = share * ncol
    cols = factor.shape[1]
    sub = cols // nrow
    slots = owner.shape[0]
    count = slots // 2
    order = [jnp.array(t, I32)[z] for t in (FAR, MIDDLE, NEAR)] + [z]

    slot = jnp.arange(slots, dtype=I32)
    same = owner[:, None] == owner[None, :]
    rank = jnp.sum((same & (slot[None, :] < slot[:, None])).astype(I32), axis=1)
    hit = (owner == z)[None, :] & (rank[None, :] == jnp.arange(capacity, dtype=I32)[:, None])
    place = jnp.sum(jnp.where(hit, inside[None, :], 0), axis=1)
    spot = jnp.stack([z ^ d for d in range(ncol)]).astype(I32)
    picked = pick(root, place, spot, ncol)
    pieces = [picked[0]] + [swap(picked[d], "col", d) for d in range(1, ncol)]
    turn = lambda x: jnp.where(g == 0, x, jnp.roll(x, count))
    selected = assemble(pieces, turn(owner) ^ z, turn(rank))

    mine = selected[:, :width]
    both = jnp.concatenate([mine, swap(selected[:, width:], "grp", 1)], axis=0)
    strip = width // nrow
    margin = row_scatter(symmetric_rows(both, both, 1, strip), r, nrow)
    half = share // 2
    rows_all = [lax.all_gather(links[h * half : (h + 1) * half], "col", axis=0) for h in (0, 1)]
    multiply = lambda h: mm(rows_all[h].reshape(width // 2, -1), factor, ((1,), (0,)))
    part_of = lambda x: row_scatter(lambda i: take(x, i * sub, sub, 1), r, nrow).astype(BF16)
    margin, first = lax.optimization_barrier((margin, multiply(0)))
    margin = col_scatter(margin, z)
    first = part_of(first)
    margin, second = lax.optimization_barrier((margin, multiply(1)))
    margin = col_gather(margin, z)
    second = part_of(second)
    solved = jnp.concatenate([first.reshape(ncol, half, sub), second.reshape(ncol, half, sub)], axis=1)
    solved = solved.reshape(width, sub)
    links_all = jnp.concatenate(rows_all, axis=1).reshape(width, -1)
    my_weights = take(weights, r * sub, sub, 0)[None, :]
    scaled = (solved.astype(F32) * my_weights).astype(BF16)
    margin = symmetric_whole(margin, strip, r, nrow)

    def pull(places):
        left = jnp.concatenate([take(margin, q * share, share, 0) for q in places], axis=0)
        part = (2.0 * mm(left, solved, ((1,), (0,))) * my_weights).astype(BF16)
        part = row_gather(part, r, nrow, 1)
        return part, mm(part, factor, ((1,), (1,))).astype(BF16)

    far, to_far = pull(order[:1])
    middle, to_middle = pull(order[1:2])
    rest, to_rest = pull(order[2:])
    grad_links = line_scatter([to_far, to_middle, to_rest[:share], to_rest[share:]], z)
    pulled = jnp.zeros((width, cols), BF16)
    for q, part in zip(order, (far, middle, rest[:share], rest[share:])):
        pulled = lax.dynamic_update_slice_in_dim(pulled, part, q * share, 0)

    grad_factor = mm(links_all, pulled, ((0,), (0,)))
    grad_factor = (grad_factor + 2.0 * factor.astype(F32) * weights[None, :]).astype(BF16)

    adjoint = row_scatter(symmetric_rows(scaled, solved, 0, strip), r, nrow)
    adjoint = symmetric_whole(col_gather(col_scatter(adjoint, z), z), strip, r, nrow)
    adjoint_other = swap(adjoint, "grp", 1)
    band_all = lax.all_gather(after(selected, rows_all[1]), "col", axis=0, tiled=True)
    base = 2.0 * root.astype(F32) * after(root_weights, margin).astype(F32)[None, :]
    here = jnp.where(owner == z, inside, -1).reshape(2, count)
    here = jnp.where(g == 0, here, here[::-1])
    match = here[:, :, None] == jnp.arange(blocks, dtype=I32)[None, None, :]
    has = jnp.any(match, axis=1)
    at = jnp.sum(jnp.where(match, jnp.arange(count, dtype=I32)[None, :, None], 0), axis=1)
    used = jnp.any(has, axis=0)
    total = jnp.sum(used.astype(I32))
    index = jnp.cumsum(used.astype(I32)) - 1
    step = jnp.minimum(jnp.arange(min(capacity, blocks), dtype=I32), jnp.maximum(total - 1, 0))
    chosen = used[None, :] & (index[None, :] == step[:, None])
    of = lambda x: jnp.sum(jnp.where(chosen, x[None, :], 0), axis=1).astype(I32)
    block = of(jnp.arange(blocks, dtype=I32))
    at = jnp.stack([of(at[w]) for w in range(2)])
    has = jnp.stack([of(has[w].astype(I32)) for w in range(2)])
    grad_root = finish(
        base.astype(BF16),
        root,
        root_weights[None, :],
        adjoint,
        adjoint_other,
        band_all,
        block,
        at,
        has,
    )
    return (grad_root, grad_factor[None], grad_links[None])


def local(root, child_inverse, coupling, child_weights, root_weights, parent_blocks):
    blocks = root.shape[1] // BW
    ids = parent_blocks.reshape(-1)
    owner, inside = ids // blocks, ids % blocks
    slots = ids.shape[0]
    usual = slots * 5 // 12
    most = jnp.max(jnp.sum((owner[:, None] == owner[None, :]).astype(I32), axis=1))
    args = (root, child_inverse, coupling, child_weights, root_weights, owner, inside)
    return lax.cond(
        most <= usual,
        functools.partial(program, usual),
        functools.partial(program, slots),
        *args,
    )


def solution(mesh):
    return jax.shard_map(
        local,
        mesh=mesh,
        in_specs=(
            P(("grp", "row"), "col"),
            P("grp", "row", "col"),
            P("grp", "col", "row"),
            P("grp", "col"),
            P("col"),
            P(),
        ),
        out_specs=(P(("grp", "row"), "col"), P("grp", "row", "col"), P("grp", "col", "row")),
        check_vma=False,
    )
```

time: 1310 us -> 642 us (0.49)
  waiting for transfers between devices: 1010 us -> 299 us
  starting transfers between devices: 1.07 us -> 103 us
  local copies, waits for them, and re-layouts: 101 us -> 41.9 us
  matrix products: 134 us -> 80.1 us
  Pallas kernels: 0 us -> 41.1 us
    all_gather x6 -> x3, waiting for transfers between devices: 391 us -> 0.02 us  [the longest x2 0.02 us: program(): lax.all_gather(links[h * half:(h + 1) * half], 'col', axis=0)]
    psum x1 -> x0, waiting for transfers between devices: 324 us -> none  [local(): selected = lax.psum(picked.astype(jnp.bfloat16), 'col')]
    ppermute x0 -> x50, waiting for transfers between devices: none -> 299 us  [the longest x44 283 us: swap(): return lax.ppermute(x, axis, [(i, i ^ d) for i in range(n)])]
    reduce_scatter x4 -> x0, waiting for transfers between devices: 295 us -> none  [the longest x1 132 us: local(): lax.psum_scatter(jnp.dot(pulled_all, factor.T, preferred_element_type=jnp...]
    ppermute x0 -> x50, starting transfers between devices: none -> 103 us  [the longest x44 93.5 us: swap(): return lax.ppermute(x, axis, [(i, i ^ d) for i in range(n)])]
    dot_general x13 -> x17, matrix products: 134 us -> 80.1 us  [mm(): lax.dot_general(a, b, (contract, ((), ())), preferred_element_type=F32)]
    unnamed x35 -> x0, local copies, waits for them, and re-layouts: 53.5 us -> none
    pallas_call x0 -> x5, Pallas kernels: none -> 41.1 us  [the longest x1 19.3 us: finish(): pl.pallas_call(finish_kernel, grid_spec=pltpu.PrefetchScalarGridSpec(num_...]
  transfers between devices with their start and end apart: 11 -> 53, of which waited for: 11 -> 25; matrix products, arithmetic and copies ran while one was open for 19% -> 25% of each run, Pallas kernels for 0% -> 3%
where the time goes in v2:
time: 642 us; the launch traced here: 632 us
  waiting for transfers between devices  299 us (47%)
  starting transfers between devices  103 us (16%)
  matrix products  80.1 us (12%)
  other arithmetic  44 us (7%)
  local copies, waits for them, and re-layouts  41.9 us (7%)
  Pallas kernels  41.1 us (6%)
  between operations  14.9 us (2%)
  loops' own time  7.13 us (1%)
    ppermute x44, waiting for transfers between devices, swap(): return lax.ppermute(x, axis, [(i, i ^ d) for i in range(n)])  283 us
    ppermute x44, starting transfers between devices, swap(): return lax.ppermute(x, axis, [(i, i ^ d) for i in range(n)])  93.5 us
    dot_general x17, matrix products, mm(): lax.dot_general(a, b, (contract, ((), ())), preferred_element_type=F32)  80.1 us
    pallas_call x1, Pallas kernels, finish(): pl.pallas_call(finish_kernel, grid_spec=pltpu.PrefetchScalarGridSpec(num_...  19.3 us
  transfers between devices with their start and end apart: 53, of which 25 were waited for; matrix products, arithmetic and copies ran while one was open for 25% of the time, Pallas kernels for 3%

profile of v2, /device:TPU:0, one launch (start us, length us, event | category | flops | bytes accessed | tf_op | source)
XLA Modules:
  0.0 631.7 jit_solution(6608748287305431227)
XLA Ops:
  10.3 614.4 %conditional.1 = (bf16[1536,3072]{1,0:T(8,128)(2,1)}, bf16[1,2048,2048]{2,1,0:T(8,128)(2,1)}, bf16[1,384,2048]{2,1,0:T(8,128)(2,1)}) conditional(s32[]{:T(128)} %convert_element_type.505, (s32[24]{0:T(128)S(1)}, s32[24]{0:T(128)S(1)}, bf16[3072]{0:T(1024)(128)(2,1)}, bf16[1536,3072]{1,0:T(8,128)(2,1)}, bf16[1,384,2048]{2,1,0:T(8,128)(2,1)}, ...), branch_computations={%region_2.15_spmd, %region_15.28_spmd} | conditional | flops 52986761216 | bytes 705793536 | solution.py:363
  13.7 2.8 fusion.183
  18.3 7.2 %branch_1_fun.5 = (bf16[384,1280]{1,0:T(8,128)(2,1)}, bf16[384,1280]{1,0:T(8,128)(2,1)}, bf16[384,1280]{1,0:T(8,128)(2,1)}, bf16[384,1280]{1,0:T(8,128)(2,1)}) custom-call(s32[10]{0:T(128)} %select_reduce_fusion.8.place, s32[4]{0:T(128)} %pad_add_fusion.5.spot, bf16[1536,3072]{1,0:T(8,128)(2,1)} %get-tuple-element.119.root_ref), custom_call_target="tpu_custom_call" | custom-call | bytes 7864320 | tf_op jit(solution)/shard_map/cond/branch_1_fun/pallas_call | solution.py:42
  25.4 3.0 collective-permute-start.50
  28.5 2.6 collective-permute-start.51
  31.8 80.4 %collective-permute-done.50.refs_1_ = bf16[384,1280]{1,0:T(8,128)(2,1)S(1)} collective-permute-done((bf16[384,1280]{1,0:T(8,128)(2,1)}, bf16[384,1280]{1,0:T(8,128)(2,1)S(1)}, u32[]{:S(2)}, u32[]{:S(2)}) %collective-permute-start.50) | collective-permute-done | bytes 983072 | tf_op jit(solution)/shard_map/cond/branch_1_fun/ppermute | solution.py:31
  112.2 8.4 %collective-permute-done.51.refs_2_ = bf16[384,1280]{1,0:T(8,128)(2,1)S(1)} collective-permute-done((bf16[384,1280]{1,0:T(8,128)(2,1)}, bf16[384,1280]{1,0:T(8,128)(2,1)S(1)}, u32[]{:S(2)}, u32[]{:S(2)}) %collective-permute-start.51) | collective-permute-done | bytes 983072 | tf_op jit(solution)/shard_map/cond/branch_1_fun/ppermute | solution.py:31
  120.6 25.1 %collective-permute-done.52.refs_3_ = bf16[384,1280]{1,0:T(8,128)(2,1)S(1)} collective-permute-done((bf16[384,1280]{1,0:T(8,128)(2,1)}, bf16[384,1280]{1,0:T(8,128)(2,1)S(1)}, u32[]{:S(2)}, u32[]{:S(2)}) %collective-permute-start.52) | collective-permute-done | bytes 983072 | tf_op jit(solution)/shard_map/cond/branch_1_fun/ppermute | solution.py:31
  146.9 3.4 branch_1_fun.6
  150.3 2.8 fusion.182
  159.1 5.6 pad_maximum_fusion.10
  172.8 11.3 %collective-permute-done.54 = bf16[384,896]{1,0:T(8,128)(2,1)S(1)} collective-permute-done((bf16[384,896]{1,0:T(8,128)(2,1)S(1)}, bf16[384,896]{1,0:T(8,128)(2,1)S(1)}, u32[]{:S(2)}, u32[]{:S(2)}) %collective-permute-start.54) | collective-permute-done | bytes 688160 | tf_op jit(solution)/shard_map/cond/branch_1_fun/ppermute | solution.py:31
  184.2 16.7 %collective-permute-done.55 = bf16[384,896]{1,0:T(8,128)(2,1)S(1)} collective-permute-done((bf16[384,896]{1,0:T(8,128)(2,1)S(1)}, bf16[384,896]{1,0:T(8,128)(2,1)S(1)}, u32[]{:S(2)}, u32[]{:S(2)}) %collective-permute-start.55) | collective-permute-done | bytes 688160 | tf_op jit(solution)/shard_map/cond/branch_1_fun/ppermute | solution.py:31
  201.2 11.7 %fusion.92 = f32[768,2048]{1,0:T(8,128)} fusion(bf16[768,2048]{1,0:T(8,128)(2,1)} %bitcast.155, bf16[1,2048,2048]{2,1,0:T(8,128)(2,1)} %get-tuple-element.123), kind=kOutput, calls=%fused_computation.211 | convolution fusion | flops 6442450944 | bytes 17825792 | tf_op jit(solution)/shard_map/cond/branch_1_fun/dot_general | solution.py:18
  213.0 36.8 %collective-permute-start.60 = (bf16[96,896]{1,0:T(8,128)(2,1)S(1)}, bf16[96,896]{1,0:T(8,128)(2,1)S(1)}, u32[]{:S(2)}, u32[]{:S(2)}) collective-permute-start(bf16[96,896]{1,0:T(8,128)(2,1)S(1)} %get-tuple-element.244), channel_id=1, source_target_pairs={{0,1},{1,0},{2,3},{3,2},{4,5},{5,4},{6,7},{7,6},{8,9},{9,8},{10,11... | collective-permute-start | bytes 516104 | tf_op jit(solution)/shard_map/cond/branch_1_fun/ppermute | solution.py:31
  249.7 2.4 collective-permute-start.62
  252.2 12.1 %fusion.90 = f32[768,2048]{1,0:T(8,128)} fusion(bf16[768,2048]{1,0:T(8,128)(2,1)} %bitcast.157, bf16[1,2048,2048]{2,1,0:T(8,128)(2,1)} %get-tuple-element.123), kind=kOutput, calls=%fused_computation.209 | convolution fusion | flops 6442450944 | bytes 17825792 | tf_op jit(solution)/shard_map/cond/branch_1_fun/dot_general | solution.py:18
  264.2 3.9 dynamic-slice_convert_fusion.17
  275.1 2.0 collective-permute-start.81
  277.1 7.7 %pad_maximum_fusion.9 = bf16[4,384,2048]{2,1,0:T(8,128)(2,1)} fusion(bf16[4,192,2048]{2,1,0:T(8,128)(2,1)} %all-gather.15.cloned.1.call-done, bf16[4,192,2048]{2,1,0:T(8,128)(2,1)} %all-gather.13.cloned.1.call-done), kind=kLoop, calls=%fused_computation.214 | loop fusion | flops 12582912 | bytes 12582912 | tf_op jit(solution)/shard_map/cond/branch_1_fun/concatenate | solution.py:300
  284.8 2.7 dynamic-slice_convert_fusion.14
  287.5 5.3 collective-permute-done.80
  296.8 8.3 %collective-permute-done.58 = bf16[768,512]{1,0:T(8,128)(2,1)S(1)} collective-permute-done((bf16[768,512]{1,0:T(8,128)(2,1)}, bf16[768,512]{1,0:T(8,128)(2,1)S(1)}, u32[]{:S(2)}, u32[]{:S(2)}) %collective-permute-start.58) | collective-permute-done | bytes 786464 | tf_op jit(solution)/shard_map/cond/branch_1_fun/ppermute | solution.py:31
  305.1 2.6 collective-permute-start.82
  307.7 2.1 collective-permute-start.83
  309.8 1.9 add_convert_fusion.17
  311.7 10.9 %collective-permute-done.63 = bf16[768,512]{1,0:T(8,128)(2,1)S(1)} collective-permute-done((bf16[768,512]{1,0:T(8,128)(2,1)S(1)}, bf16[768,512]{1,0:T(8,128)(2,1)S(1)}, u32[]{:S(2)}, u32[]{:S(2)}) %collective-permute-start.63) | collective-permute-done | bytes 786464 | tf_op jit(solution)/shard_map/cond/branch_1_fun/ppermute | solution.py:31
  324.1 14.6 %collective-permute-done.64 = bf16[768,512]{1,0:T(8,128)(2,1)S(1)} collective-permute-done((bf16[768,512]{1,0:T(8,128)(2,1)S(1)}, bf16[768,512]{1,0:T(8,128)(2,1)S(1)}, u32[]{:S(2)}, u32[]{:S(2)}) %collective-permute-start.64) | collective-permute-done | bytes 786464 | tf_op jit(solution)/shard_map/cond/branch_1_fun/ppermute | solution.py:31
  340.4 1.8 add_convert_fusion.16
  354.4 10.8 %collective-permute-done.83 = bf16[384,896]{1,0:T(8,128)(2,1)S(1)} collective-permute-done((bf16[384,896]{1,0:T(8,128)(2,1)S(1)}, bf16[384,896]{1,0:T(8,128)(2,1)S(1)}, u32[]{:S(2)}, u32[]{:S(2)}) %collective-permute-start.83) | collective-permute-done | bytes 688160 | tf_op jit(solution)/shard_map/cond/branch_1_fun/ppermute | solution.py:31
  365.2 4.7 collective-permute-done.84
  370.0 5.6 branch_1_fun.8
  375.9 2.8 constant_dynamic-update-slice_fusion.38
  379.8 2.3 collective-permute-start.90
  383.5 2.9 constant_dynamic-update-slice_fusion.43
  387.0 10.1 %multiply_convert_fusion.3.base = bf16[1536,3072]{1,0:T(8,128)(2,1)} fusion(bf16[1536,3072]{1,0:T(8,128)(2,1)} %get-tuple-element.119.root_ref, f32[3072]{0:T(1024)S(1)} %convert_multiply_fusion.1), kind=kLoop, calls=%fused_computation.201 | loop fusion | flops 14155776 | bytes 18886656 | tf_op jit(solution)/shard_map/cond/branch_1_fun/convert_element_type | solution.py:342
  399.3 2.3 constant_dynamic-update-slice_fusion.33
  403.2 2.3 collective-permute-start.87
  412.4 24.6 %collective-permute-done.86 = bf16[384,512]{1,0:T(8,128)(2,1)S(1)} collective-permute-done((bf16[384,512]{1,0:T(8,128)(2,1)}, bf16[384,512]{1,0:T(8,128)(2,1)S(1)}, u32[]{:S(2)}, u32[]{:S(2)}) %collective-permute-start.86) | collective-permute-done | bytes 393248 | tf_op jit(solution)/shard_map/cond/branch_1_fun/ppermute | solution.py:31
  440.1 3.5 fusion.98
  443.6 5.0 fusion.101
  448.6 2.0 collective-permute-start.93
  450.7 17.9 %collective-permute-done.67 = bf16[384,896]{1,0:T(8,128)(2,1)S(1)} collective-permute-done((bf16[384,896]{1,0:T(8,128)(2,1)S(1)}, bf16[384,896]{1,0:T(8,128)(2,1)S(1)}, u32[]{:S(2)}, u32[]{:S(2)}) %collective-permute-start.67) | collective-permute-done | bytes 688160 | tf_op jit(solution)/shard_map/cond/branch_1_fun/ppermute | solution.py:31
  471.1 3.6 broadcast.151
  474.8 2.8 constant_dynamic-update-slice_fusion.39
  478.6 2.4 collective-permute-start.71
  482.3 3.8 collective-permute-done.70
  486.1 2.7 collective-permute-start.94
  491.5 3.3 collective-permute-start.73
  495.9 9.1 %fusion.95 = bf16[768,2048]{1,0:T(8,128)(2,1)S(1)} fusion(bf16[768,2048]{1,0:T(8,128)(2,1)S(1)} %constant_dynamic-update-slice_fusion.30, bf16[1,2048,2048]{2,1,0:T(8,128)(2,1)} %get-tuple-element.123), kind=kOutput, calls=%fused_computation.230 | convolution fusion | flops 6444023808 | bytes 14680064 | tf_op jit(solution)/shard_map/cond/branch_1_fun/dot_general | solution.py:18
  505.0 9.9 %collective-permute-done.72 = bf16[96,896]{1,0:T(8,128)(2,1)S(1)} collective-permute-done((bf16[96,896]{1,0:T(8,128)(2,1)S(1)}, bf16[96,896]{1,0:T(8,128)(2,1)S(1)}, u32[]{:S(2)}, u32[]{:S(2)}) %collective-permute-start.72) | collective-permute-done | bytes 172064 | tf_op jit(solution)/shard_map/cond/branch_1_fun/ppermute | solution.py:31
  514.9 3.7 collective-permute-done.73
  518.6 11.0 %collective-permute-done.74 = bf16[96,896]{1,0:T(8,128)(2,1)S(1)} collective-permute-done((bf16[96,896]{1,0:T(8,128)(2,1)S(1)}, bf16[96,896]{1,0:T(8,128)(2,1)S(1)}, u32[]{:S(2)}, u32[]{:S(2)}) %collective-permute-start.74) | collective-permute-done | bytes 172064 | tf_op jit(solution)/shard_map/cond/branch_1_fun/ppermute | solution.py:31
  531.2 3.2 collective-permute-start.76
  537.2 1.8 collective-permute-start.98
  540.8 9.9 %collective-permute-done.76 = bf16[384,896]{1,0:T(8,128)(2,1)S(1)} collective-permute-done((bf16[384,896]{1,0:T(8,128)(2,1)S(1)}, bf16[384,896]{1,0:T(8,128)(2,1)S(1)}, u32[]{:S(2)}, u32[]{:S(2)}) %collective-permute-start.76) | collective-permute-done | bytes 688160 | tf_op jit(solution)/shard_map/cond/branch_1_fun/ppermute | solution.py:31
  550.8 5.6 branch_1_fun.7.mine_ref
  557.8 2.9 add_convert_fusion.14
  563.7 21.3 %fusion.94 = bf16[1,2048,2048]{2,1,0:T(8,128)(2,1)} fusion(f32[2048]{0:T(1024)S(1)} %bitcast.171, bf16[1,2048,2048]{2,1,0:T(8,128)(2,1)} %get-tuple-element.123, bf16[1536,2048]{1,0:T(8,128)(2,1)} %bitcast.139, bf16[1536,2048]{1,0:T(8,128)(2,1)} %slice_dynamic-update-slice_fusion.2), kind=kOutput, calls=%fused_computation.213 | convolution fusion | flops 12901679104 | bytes 29368320 | tf_op jit(solution)/shard_map/cond/branch_1_fun/dot_general | solution.py:18
  584.9 11.6 %collective-permute-done.96 = bf16[384,2048]{1,0:T(8,128)(2,1)S(1)} collective-permute-done((bf16[384,2048]{1,0:T(8,128)(2,1)S(1)}, bf16[384,2048]{1,0:T(8,128)(2,1)S(1)}, u32[]{:S(2)}, u32[]{:S(2)}) %collective-permute-start.96) | collective-permute-done | bytes 1572896 | tf_op jit(solution)/shard_map/cond/branch_1_fun/ppermute | solution.py:170
  596.6 4.2 collective-permute-done.99
  600.8 2.0 fusion.112
  602.8 2.3 copy-done.1
  605.1 19.3 %branch_1_fun.9 = bf16[1536,3072]{1,0:T(8,128)(2,1)} custom-call(s32[10]{0:T(128)S(1)} %get-tuple-element.149.block, s32[2,10]{1,0:T(2,128)S(1)} %get-tuple-element.286.at, s32[2,10]{1,0:T(2,128)S(1)} %get-tuple-element.287.has, bf16[1536,3072]{1,0:T(8,128)(2,1)} %get-tuple-element.119.root_ref, ...), custom_call_target="tpu_custom_call", output_to_operand_aliasing={{}: (8, {})} | custom-call | flops 7247757312 | bytes 18874368 | tf_op jit(solution)/shard_map/cond/branch_1_fun/pallas_call | solution.py:140
  (209 shorter events, 80.1 us)
Async XLA Ops:
  13.7 187.5 %all-gather.13.cloned.1.call-start = ((), (), s32[]{:S(2)}) async-start(), calls=%async_computation.3 | async-start | bytes 3932160 | tf_op jit(solution)/shard_map/cond/branch_1_fun/all_gather | solution.py:289
  16.5 235.7 %all-gather.15.cloned.1.call-start = ((), (), s32[]{:S(2)}) async-start(), calls=%async_computation.4 | async-start | bytes 3932160 | tf_op jit(solution)/shard_map/cond/branch_1_fun/all_gather | solution.py:289
  25.4 86.8 %collective-permute-start.50 = (bf16[384,1280]{1,0:T(8,128)(2,1)}, bf16[384,1280]{1,0:T(8,128)(2,1)S(1)}, u32[]{:S(2)}, u32[]{:S(2)}) collective-permute-start(bf16[384,1280]{1,0:T(8,128)(2,1)} %get-tuple-element.65), channel_id=1, source_target_pairs={{0,1},{1,0},{2,3},{3,2},{4,5},{5,4},{6,7},{7,6},{8,9},{9,8},{10,11... | collective-permute-start | bytes 2949128 | tf_op jit(solution)/shard_map/cond/branch_1_fun/ppermute | solution.py:31
  28.5 92.1 %collective-permute-start.51 = (bf16[384,1280]{1,0:T(8,128)(2,1)}, bf16[384,1280]{1,0:T(8,128)(2,1)S(1)}, u32[]{:S(2)}, u32[]{:S(2)}) collective-permute-start(bf16[384,1280]{1,0:T(8,128)(2,1)} %get-tuple-element.66), channel_id=1, source_target_pairs={{0,2},{1,3},{2,0},{3,1},{4,6},{5,7},{6,4},{7,5},{8,10},{9,11},{10,... | collective-permute-start | bytes 2949128 | tf_op jit(solution)/shard_map/cond/branch_1_fun/ppermute | solution.py:31
  31.1 114.6 %collective-permute-start.52 = (bf16[384,1280]{1,0:T(8,128)(2,1)}, bf16[384,1280]{1,0:T(8,128)(2,1)S(1)}, u32[]{:S(2)}, u32[]{:S(2)}) collective-permute-start(bf16[384,1280]{1,0:T(8,128)(2,1)} %get-tuple-element.67), channel_id=1, source_target_pairs={{0,3},{1,2},{2,1},{3,0},{4,7},{5,6},{6,5},{7,4},{8,11},{9,10},{10,... | collective-permute-start | bytes 2949128 | tf_op jit(solution)/shard_map/cond/branch_1_fun/ppermute | solution.py:31
  31.4 571.4 %all-gather.17.cloned.1.call-start = ((), (), s32[]{:S(2)}) async-start(), calls=%async_computation.5 | async-start | bytes 11796480 | tf_op jit(solution)/shard_map/cond/branch_1_fun/all_gather | solution.py:325
  150.3 3.5 copy-start.22
  150.3 4.7 copy-start.20
  150.3 6.0 copy-start.18
  150.3 7.3 %copy-start.14 = (bf16[1,2048]{1,0:T(2,128)(2,1)S(1)}, bf16[1,2048]{1,0:T(2,128)(2,1)}, u32[]{:S(2)}) copy-start(bf16[1,2048]{1,0:T(2,128)(2,1)} %get-tuple-element.125) | copy-start | bytes 12292 | tf_op jit(solution)/shard_map/cond
  150.3 8.1 %copy-start.16 = (bf16[3072]{0:T(1024)(128)(2,1)S(1)}, bf16[3072]{0:T(1024)(128)(2,1)}, u32[]{:S(2)}) copy-start(bf16[3072]{0:T(1024)(128)(2,1)} %get-tuple-element.76) | copy-start | bytes 18436 | tf_op jit(solution)/shard_map/cond
  153.1 5.9 collective-permute-start.53
  165.9 18.3 %collective-permute-start.54 = (bf16[384,896]{1,0:T(8,128)(2,1)S(1)}, bf16[384,896]{1,0:T(8,128)(2,1)S(1)}, u32[]{:S(2)}, u32[]{:S(2)}) collective-permute-start(bf16[384,896]{1,0:T(8,128)(2,1)S(1)} %pad_maximum_fusion.12), channel_id=1, source_target_pairs={{0,4},{4,0},{8,12},{12,8},{1,5},{5,1},{9,13},{13,9},{2,6},{6,2},{1... | collective-permute-start | bytes 2064392 | tf_op jit(solution)/shard_map/cond/branch_1_fun/ppermute | solution.py:31
  168.5 32.4 %collective-permute-start.55 = (bf16[384,896]{1,0:T(8,128)(2,1)S(1)}, bf16[384,896]{1,0:T(8,128)(2,1)S(1)}, u32[]{:S(2)}, u32[]{:S(2)}) collective-permute-start(bf16[384,896]{1,0:T(8,128)(2,1)S(1)} %pad_maximum_fusion.13), channel_id=1, source_target_pairs={{0,8},{4,12},{8,0},{12,4},{1,9},{5,13},{9,1},{13,5},{2,10},{6,14},... | collective-permute-start | bytes 2064392 | tf_op jit(solution)/shard_map/cond/branch_1_fun/ppermute | solution.py:31
  171.1 29.7 %collective-permute-start.56 = (bf16[384,896]{1,0:T(8,128)(2,1)S(1)}, bf16[384,896]{1,0:T(8,128)(2,1)S(1)}, u32[]{:S(2)}, u32[]{:S(2)}) collective-permute-start(bf16[384,896]{1,0:T(8,128)(2,1)S(1)} %pad_maximum_fusion.14), channel_id=1, source_target_pairs={{0,12},{4,8},{8,4},{12,0},{1,13},{5,9},{9,5},{13,1},{2,14},{6,10},... | collective-permute-start | bytes 2064392 | tf_op jit(solution)/shard_map/cond/branch_1_fun/ppermute | solution.py:31
  213.0 55.8 %collective-permute-start.60 = (bf16[96,896]{1,0:T(8,128)(2,1)S(1)}, bf16[96,896]{1,0:T(8,128)(2,1)S(1)}, u32[]{:S(2)}, u32[]{:S(2)}) collective-permute-start(bf16[96,896]{1,0:T(8,128)(2,1)S(1)} %get-tuple-element.244), channel_id=1, source_target_pairs={{0,1},{1,0},{2,3},{3,2},{4,5},{5,4},{6,7},{7,6},{8,9},{9,8},{10,11... | collective-permute-start | bytes 516104 | tf_op jit(solution)/shard_map/cond/branch_1_fun/ppermute | solution.py:31
  249.7 19.0 %collective-permute-start.61 = (bf16[96,896]{1,0:T(8,128)(2,1)S(1)}, bf16[96,896]{1,0:T(8,128)(2,1)S(1)}, u32[]{:S(2)}, u32[]{:S(2)}) collective-permute-start(bf16[96,896]{1,0:T(8,128)(2,1)S(1)} %get-tuple-element.246), channel_id=1, source_target_pairs={{0,2},{1,3},{2,0},{3,1},{4,6},{5,7},{6,4},{7,5},{8,10},{9,11},{10,... | collective-permute-start | bytes 516104 | tf_op jit(solution)/shard_map/cond/branch_1_fun/ppermute | solution.py:31
  249.7 19.0 %collective-permute-start.62 = (bf16[96,896]{1,0:T(8,128)(2,1)S(1)}, bf16[96,896]{1,0:T(8,128)(2,1)S(1)}, u32[]{:S(2)}, u32[]{:S(2)}) collective-permute-start(bf16[96,896]{1,0:T(8,128)(2,1)S(1)} %get-tuple-element.245), channel_id=1, source_target_pairs={{0,3},{1,2},{2,1},{3,0},{4,7},{5,6},{6,5},{7,4},{8,11},{9,10},{10,... | collective-permute-start | bytes 516104 | tf_op jit(solution)/shard_map/cond/branch_1_fun/ppermute | solution.py:31
  268.2 27.3 %collective-permute-start.57 = (bf16[768,512]{1,0:T(8,128)(2,1)}, bf16[768,512]{1,0:T(8,128)(2,1)S(1)}, u32[]{:S(2)}, u32[]{:S(2)}) collective-permute-start(bf16[768,512]{1,0:T(8,128)(2,1)} %get-tuple-element.225), channel_id=1, source_target_pairs={{0,4},{4,0},{8,12},{12,8},{1,5},{5,1},{9,13},{13,9},{2,6},{6,2},{1... | collective-permute-start | bytes 2359304 | tf_op jit(solution)/shard_map/cond/branch_1_fun/ppermute | solution.py:31
  268.8 6.3 collective-permute-start.79
  270.0 35.2 %collective-permute-start.58 = (bf16[768,512]{1,0:T(8,128)(2,1)}, bf16[768,512]{1,0:T(8,128)(2,1)S(1)}, u32[]{:S(2)}, u32[]{:S(2)}) collective-permute-start(bf16[768,512]{1,0:T(8,128)(2,1)} %get-tuple-element.227), channel_id=1, source_target_pairs={{0,8},{4,12},{8,0},{12,4},{1,9},{5,13},{9,1},{13,5},{2,10},{6,14},... | collective-permute-start | bytes 2359304 | tf_op jit(solution)/shard_map/cond/branch_1_fun/ppermute | solution.py:31
  271.4 36.3 %collective-permute-start.59 = (bf16[768,512]{1,0:T(8,128)(2,1)}, bf16[768,512]{1,0:T(8,128)(2,1)S(1)}, u32[]{:S(2)}, u32[]{:S(2)}) collective-permute-start(bf16[768,512]{1,0:T(8,128)(2,1)} %get-tuple-element.226), channel_id=1, source_target_pairs={{0,12},{4,8},{8,4},{12,0},{1,13},{5,9},{9,5},{13,1},{2,14},{6,10},... | collective-permute-start | bytes 2359304 | tf_op jit(solution)/shard_map/cond/branch_1_fun/ppermute | solution.py:31
  272.9 19.9 %collective-permute-start.80 = (bf16[96,896]{1,0:T(8,128)(2,1)S(1)}, bf16[96,896]{1,0:T(8,128)(2,1)S(1)}, u32[]{:S(2)}, u32[]{:S(2)}) collective-permute-start(bf16[96,896]{1,0:T(8,128)(2,1)S(1)} %add_convert_fusion.19), channel_id=1, source_target_pairs={{0,2},{1,3},{2,0},{3,1},{4,6},{5,7},{6,4},{7,5},{8,10},{9,11},{10,... | collective-permute-start | bytes 516104 | tf_op jit(solution)/shard_map/cond/branch_1_fun/ppermute | solution.py:31
  275.1 18.9 %collective-permute-start.81 = (bf16[96,896]{1,0:T(8,128)(2,1)S(1)}, bf16[96,896]{1,0:T(8,128)(2,1)S(1)}, u32[]{:S(2)}, u32[]{:S(2)}) collective-permute-start(bf16[96,896]{1,0:T(8,128)(2,1)S(1)} %add_convert_fusion.19), channel_id=1, source_target_pairs={{0,3},{1,2},{2,1},{3,0},{4,7},{5,6},{6,5},{7,4},{8,11},{9,10},{10,... | collective-permute-start | bytes 516104 | tf_op jit(solution)/shard_map/cond/branch_1_fun/ppermute | solution.py:31
  292.8 29.8 %collective-permute-start.63 = (bf16[768,512]{1,0:T(8,128)(2,1)S(1)}, bf16[768,512]{1,0:T(8,128)(2,1)S(1)}, u32[]{:S(2)}, u32[]{:S(2)}) collective-permute-start(bf16[768,512]{1,0:T(8,128)(2,1)S(1)} %get-tuple-element.228), channel_id=1, source_target_pairs={{0,4},{4,0},{8,12},{12,8},{1,5},{5,1},{9,13},{13,9},{2,6},{6,2},{1... | collective-permute-start | bytes 2359304 | tf_op jit(solution)/shard_map/cond/branch_1_fun/ppermute | solution.py:31
  294.0 44.7 %collective-permute-start.64 = (bf16[768,512]{1,0:T(8,128)(2,1)S(1)}, bf16[768,512]{1,0:T(8,128)(2,1)S(1)}, u32[]{:S(2)}, u32[]{:S(2)}) collective-permute-start(bf16[768,512]{1,0:T(8,128)(2,1)S(1)} %get-tuple-element.230), channel_id=1, source_target_pairs={{0,8},{4,12},{8,0},{12,4},{1,9},{5,13},{9,1},{13,5},{2,10},{6,14},... | collective-permute-start | bytes 2359304 | tf_op jit(solution)/shard_map/cond/branch_1_fun/ppermute | solution.py:31
  295.4 45.0 %collective-permute-start.65 = (bf16[768,512]{1,0:T(8,128)(2,1)S(1)}, bf16[768,512]{1,0:T(8,128)(2,1)S(1)}, u32[]{:S(2)}, u32[]{:S(2)}) collective-permute-start(bf16[768,512]{1,0:T(8,128)(2,1)S(1)} %get-tuple-element.229), channel_id=1, source_target_pairs={{0,12},{4,8},{8,4},{12,0},{1,13},{5,9},{9,5},{13,1},{2,14},{6,10},... | collective-permute-start | bytes 2359304 | tf_op jit(solution)/shard_map/cond/branch_1_fun/ppermute | solution.py:31
  305.1 49.2 %collective-permute-start.82 = (bf16[384,896]{1,0:T(8,128)(2,1)S(1)}, bf16[384,896]{1,0:T(8,128)(2,1)S(1)}, u32[]{:S(2)}, u32[]{:S(2)}) collective-permute-start(bf16[384,896]{1,0:T(8,128)(2,1)S(1)} %constant_dynamic-update-slice_fusion.48), channel_id=1, source_target_pairs={{0,4},{4,0},{8,12},{12,8},{1,5},{5,1},{9,13},{13,9},{2,6},{6,2},{1... | collective-permute-start | bytes 2064392 | tf_op jit(solution)/shard_map/cond/branch_1_fun/ppermute | solution.py:31
  307.7 57.4 %collective-permute-start.83 = (bf16[384,896]{1,0:T(8,128)(2,1)S(1)}, bf16[384,896]{1,0:T(8,128)(2,1)S(1)}, u32[]{:S(2)}, u32[]{:S(2)}) collective-permute-start(bf16[384,896]{1,0:T(8,128)(2,1)S(1)} %constant_dynamic-update-slice_fusion.48), channel_id=1, source_target_pairs={{0,8},{4,12},{8,0},{12,4},{1,9},{5,13},{9,1},{13,5},{2,10},{6,14},... | collective-permute-start | bytes 2064392 | tf_op jit(solution)/shard_map/cond/branch_1_fun/ppermute | solution.py:31
  322.6 47.3 %collective-permute-start.84 = (bf16[384,896]{1,0:T(8,128)(2,1)S(1)}, bf16[384,896]{1,0:T(8,128)(2,1)S(1)}, u32[]{:S(2)}, u32[]{:S(2)}) collective-permute-start(bf16[384,896]{1,0:T(8,128)(2,1)S(1)} %constant_dynamic-update-slice_fusion.48), channel_id=1, source_target_pairs={{0,12},{4,8},{8,4},{12,0},{1,13},{5,9},{9,5},{13,1},{2,14},{6,10},... | collective-permute-start | bytes 2064392 | tf_op jit(solution)/shard_map/cond/branch_1_fun/ppermute | solution.py:31
  348.0 100.6 %collective-permute-start.66 = (bf16[384,896]{1,0:T(8,128)(2,1)}, bf16[384,896]{1,0:T(8,128)(2,1)}, u32[]{:S(2)}, u32[]{:S(2)}) collective-permute-start(bf16[384,896]{1,0:T(8,128)(2,1)} %pad_maximum_fusion.15), channel_id=1, source_target_pairs={{0,4},{4,0},{8,12},{12,8},{1,5},{5,1},{9,13},{13,9},{2,6},{6,2},{1... | collective-permute-start | bytes 2064392 | tf_op jit(solution)/shard_map/cond/branch_1_fun/ppermute | solution.py:31
  378.7 22.9 %collective-permute-start.88 = (bf16[384,512]{1,0:T(8,128)(2,1)}, bf16[384,512]{1,0:T(8,128)(2,1)}, u32[]{:S(2)}, u32[]{:S(2)}) collective-permute-start(bf16[384,512]{1,0:T(8,128)(2,1)} %get-tuple-element.283), channel_id=1, source_target_pairs={{0,4},{4,0},{8,12},{12,8},{1,5},{5,1},{9,13},{13,9},{2,6},{6,2},{1... | collective-permute-start | bytes 1179656 | tf_op jit(solution)/shard_map/cond/branch_1_fun/ppermute | solution.py:31
  379.3 24.0 %collective-permute-start.89 = (bf16[384,512]{1,0:T(8,128)(2,1)}, bf16[384,512]{1,0:T(8,128)(2,1)}, u32[]{:S(2)}, u32[]{:S(2)}) collective-permute-start(bf16[384,512]{1,0:T(8,128)(2,1)} %get-tuple-element.283), channel_id=1, source_target_pairs={{0,8},{4,12},{8,0},{12,4},{1,9},{5,13},{9,1},{13,5},{2,10},{6,14},... | collective-permute-start | bytes 1179656 | tf_op jit(solution)/shard_map/cond/branch_1_fun/ppermute | solution.py:31
  379.8 26.8 %collective-permute-start.90 = (bf16[384,512]{1,0:T(8,128)(2,1)}, bf16[384,512]{1,0:T(8,128)(2,1)}, u32[]{:S(2)}, u32[]{:S(2)}) collective-permute-start(bf16[384,512]{1,0:T(8,128)(2,1)} %get-tuple-element.283), channel_id=1, source_target_pairs={{0,12},{4,8},{8,4},{12,0},{1,13},{5,9},{9,5},{13,1},{2,14},{6,10},... | collective-permute-start | bytes 1179656 | tf_op jit(solution)/shard_map/cond/branch_1_fun/ppermute | solution.py:31
  386.4 22.8 %collective-permute-start.85 = (bf16[384,512]{1,0:T(8,128)(2,1)}, bf16[384,512]{1,0:T(8,128)(2,1)}, u32[]{:S(2)}, u32[]{:S(2)}) collective-permute-start(bf16[384,512]{1,0:T(8,128)(2,1)} %get-tuple-element.281), channel_id=1, source_target_pairs={{0,4},{4,0},{8,12},{12,8},{1,5},{5,1},{9,13},{13,9},{2,6},{6,2},{1... | collective-permute-start | bytes 1179656 | tf_op jit(solution)/shard_map/cond/branch_1_fun/ppermute | solution.py:31
  398.9 41.2 %slice-start.2 = ((s8[8388608]{0:T(1024)(128)(4,1)}), s8[4194304]{0:T(1024)(128)(4,1)S(1)}, s32[]{:S(2)}) async-start(s8[8388608]{0:T(1024)(128)(4,1)} %bitcast.182), calls=%async_computation.8 | async-start | bytes 8388608 | tf_op jit(solution)/shard_map/cond
  399.3 40.8 %slice-start.3 = ((s8[8388608]{0:T(1024)(128)(4,1)}), s8[4194304]{0:T(1024)(128)(4,1)S(1)}, s32[]{:S(2)}) async-start(s8[8388608]{0:T(1024)(128)(4,1)} %bitcast.182), calls=%async_computation.9 | async-start | bytes 8388608 | tf_op jit(solution)/shard_map/cond
  401.6 5.0 copy-start.10
  401.6 7.6 %copy-start.12 = (bf16[384,896]{1,0:T(8,128)(2,1)S(1)}, bf16[384,896]{1,0:T(8,128)(2,1)}, u32[]{:S(2)}) copy-start(bf16[384,896]{1,0:T(8,128)(2,1)} %pad_maximum_fusion.17) | copy-start | bytes 2064388 | tf_op jit(solution)/shard_map/cond
  401.6 35.4 %collective-permute-start.86 = (bf16[384,512]{1,0:T(8,128)(2,1)}, bf16[384,512]{1,0:T(8,128)(2,1)S(1)}, u32[]{:S(2)}, u32[]{:S(2)}) collective-permute-start(bf16[384,512]{1,0:T(8,128)(2,1)} %get-tuple-element.281), channel_id=1, source_target_pairs={{0,8},{4,12},{8,0},{12,4},{1,9},{5,13},{9,1},{13,5},{2,10},{6,14},... | collective-permute-start | bytes 1179656 | tf_op jit(solution)/shard_map/cond/branch_1_fun/ppermute | solution.py:31
  403.2 35.7 %collective-permute-start.87 = (bf16[384,512]{1,0:T(8,128)(2,1)}, bf16[384,512]{1,0:T(8,128)(2,1)S(1)}, u32[]{:S(2)}, u32[]{:S(2)}) collective-permute-start(bf16[384,512]{1,0:T(8,128)(2,1)} %get-tuple-element.281), channel_id=1, source_target_pairs={{0,12},{4,8},{8,4},{12,0},{1,13},{5,9},{9,5},{13,1},{2,14},{6,10},... | collective-permute-start | bytes 1179656 | tf_op jit(solution)/shard_map/cond/branch_1_fun/ppermute | solution.py:31
  406.6 62.0 %collective-permute-start.67 = (bf16[384,896]{1,0:T(8,128)(2,1)S(1)}, bf16[384,896]{1,0:T(8,128)(2,1)S(1)}, u32[]{:S(2)}, u32[]{:S(2)}) collective-permute-start(bf16[384,896]{1,0:T(8,128)(2,1)S(1)} %copy-done.10), channel_id=1, source_target_pairs={{0,8},{4,12},{8,0},{12,4},{1,9},{5,13},{9,1},{13,5},{2,10},{6,14},... | collective-permute-start | bytes 2064392 | tf_op jit(solution)/shard_map/cond/branch_1_fun/ppermute | solution.py:31
  409.2 59.4 %collective-permute-start.68 = (bf16[384,896]{1,0:T(8,128)(2,1)S(1)}, bf16[384,896]{1,0:T(8,128)(2,1)S(1)}, u32[]{:S(2)}, u32[]{:S(2)}) collective-permute-start(bf16[384,896]{1,0:T(8,128)(2,1)S(1)} %copy-done.12), channel_id=1, source_target_pairs={{0,12},{4,8},{8,4},{12,0},{1,13},{5,9},{9,5},{13,1},{2,14},{6,10},... | collective-permute-start | bytes 2064392 | tf_op jit(solution)/shard_map/cond/branch_1_fun/ppermute | solution.py:31
  437.0 53.9 %collective-permute-start.91 = (bf16[768,512]{1,0:T(8,128)(2,1)}, bf16[768,512]{1,0:T(8,128)(2,1)S(1)}, u32[]{:S(2)}, u32[]{:S(2)}) collective-permute-start(bf16[768,512]{1,0:T(8,128)(2,1)} %get-tuple-element.285), channel_id=1, source_target_pairs={{0,4},{4,0},{8,12},{12,8},{1,5},{5,1},{9,13},{13,9},{2,6},{6,2},{1... | collective-permute-start | bytes 2359304 | tf_op jit(solution)/shard_map/cond/branch_1_fun/ppermute | solution.py:31
  438.9 52.6 %collective-permute-start.92 = (bf16[768,512]{1,0:T(8,128)(2,1)}, bf16[768,512]{1,0:T(8,128)(2,1)S(1)}, u32[]{:S(2)}, u32[]{:S(2)}) collective-permute-start(bf16[768,512]{1,0:T(8,128)(2,1)} %get-tuple-element.285), channel_id=1, source_target_pairs={{0,8},{4,12},{8,0},{12,4},{1,9},{5,13},{9,1},{13,5},{2,10},{6,14},... | collective-permute-start | bytes 2359304 | tf_op jit(solution)/shard_map/cond/branch_1_fun/ppermute | solution.py:31
  443.6 25.1 %copy-start.7 = (bf16[128,896]{1,0:T(8,128)(2,1)S(1)}, bf16[128,896]{1,0:T(8,128)(2,1)}, u32[]{:S(2)}) copy-start(bf16[128,896]{1,0:T(8,128)(2,1)} %get-tuple-element.248) | copy-start | bytes 688132 | tf_op jit(solution)/shard_map/cond
  443.6 25.1 %copy-start.8 = (bf16[128,896]{1,0:T(8,128)(2,1)S(1)}, bf16[128,896]{1,0:T(8,128)(2,1)}, u32[]{:S(2)}) copy-start(bf16[128,896]{1,0:T(8,128)(2,1)} %get-tuple-element.249) | copy-start | bytes 688132 | tf_op jit(solution)/shard_map/cond
  448.6 46.3 %collective-permute-start.93 = (bf16[768,512]{1,0:T(8,128)(2,1)}, bf16[768,512]{1,0:T(8,128)(2,1)S(1)}, u32[]{:S(2)}, u32[]{:S(2)}) collective-permute-start(bf16[768,512]{1,0:T(8,128)(2,1)} %get-tuple-element.285), channel_id=1, source_target_pairs={{0,12},{4,8},{8,4},{12,0},{1,13},{5,9},{9,5},{13,1},{2,14},{6,10},... | collective-permute-start | bytes 2359304 | tf_op jit(solution)/shard_map/cond/branch_1_fun/ppermute | solution.py:31
  470.1 8.4 %collective-permute-start.69 = (bf16[96,896]{1,0:T(8,128)(2,1)S(1)}, bf16[96,896]{1,0:T(8,128)(2,1)S(1)}, u32[]{:S(2)}, u32[]{:S(2)}) collective-permute-start(bf16[96,896]{1,0:T(8,128)(2,1)S(1)} %get-tuple-element.241), channel_id=1, source_target_pairs={{0,1},{1,0},{2,3},{3,2},{4,5},{5,4},{6,7},{7,6},{8,9},{9,8},{10,11... | collective-permute-start | bytes 516104 | tf_op jit(solution)/shard_map/cond/branch_1_fun/ppermute | solution.py:31
  477.5 8.6 %collective-permute-start.70 = (bf16[96,896]{1,0:T(8,128)(2,1)S(1)}, bf16[96,896]{1,0:T(8,128)(2,1)S(1)}, u32[]{:S(2)}, u32[]{:S(2)}) collective-permute-start(bf16[96,896]{1,0:T(8,128)(2,1)S(1)} %get-tuple-element.243), channel_id=1, source_target_pairs={{0,2},{1,3},{2,0},{3,1},{4,6},{5,7},{6,4},{7,5},{8,10},{9,11},{10,... | collective-permute-start | bytes 516104 | tf_op jit(solution)/shard_map/cond/branch_1_fun/ppermute | solution.py:31
  478.6 11.4 %collective-permute-start.71 = (bf16[96,896]{1,0:T(8,128)(2,1)S(1)}, bf16[96,896]{1,0:T(8,128)(2,1)S(1)}, u32[]{:S(2)}, u32[]{:S(2)}) collective-permute-start(bf16[96,896]{1,0:T(8,128)(2,1)S(1)} %get-tuple-element.242), channel_id=1, source_target_pairs={{0,3},{1,2},{2,1},{3,0},{4,7},{5,6},{6,5},{7,4},{8,11},{9,10},{10,... | collective-permute-start | bytes 516104 | tf_op jit(solution)/shard_map/cond/branch_1_fun/ppermute | solution.py:31
  486.1 48.2 %collective-permute-start.94 = (bf16[384,2048]{1,0:T(8,128)(2,1)S(1)}, bf16[384,2048]{1,0:T(8,128)(2,1)S(1)}, u32[]{:S(2)}, u32[]{:S(2)}) collective-permute-start(bf16[384,2048]{1,0:T(8,128)(2,1)S(1)} %fusion.101), channel_id=1, source_target_pairs={{0,1},{4,5},{8,9},{12,13},{16,17},{20,21},{24,25},{28,29}} | collective-permute-start | bytes 4718600 | tf_op jit(solution)/shard_map/cond/branch_1_fun/ppermute | solution.py:170
  490.0 44.3 %collective-permute-start.97 = (bf16[384,2048]{1,0:T(8,128)(2,1)S(1)}, bf16[384,2048]{1,0:T(8,128)(2,1)S(1)}, u32[]{:S(2)}, u32[]{:S(2)}) collective-permute-start(bf16[384,2048]{1,0:T(8,128)(2,1)S(1)} %fusion.101), channel_id=1, source_target_pairs={{3,2},{7,6},{11,10},{15,14},{19,18},{23,22},{27,26},{31,30}} | collective-permute-start | bytes 4718600 | tf_op jit(solution)/shard_map/cond/branch_1_fun/ppermute | solution.py:174
  490.9 24.0 %collective-permute-start.72 = (bf16[96,896]{1,0:T(8,128)(2,1)S(1)}, bf16[96,896]{1,0:T(8,128)(2,1)S(1)}, u32[]{:S(2)}, u32[]{:S(2)}) collective-permute-start(bf16[96,896]{1,0:T(8,128)(2,1)S(1)} %get-tuple-element.158), channel_id=1, source_target_pairs={{0,1},{1,0},{2,3},{3,2},{4,5},{5,4},{6,7},{7,6},{8,9},{9,8},{10,11... | collective-permute-start | bytes 516104 | tf_op jit(solution)/shard_map/cond/branch_1_fun/ppermute | solution.py:31
  491.5 27.1 %collective-permute-start.73 = (bf16[96,896]{1,0:T(8,128)(2,1)S(1)}, bf16[96,896]{1,0:T(8,128)(2,1)S(1)}, u32[]{:S(2)}, u32[]{:S(2)}) collective-permute-start(bf16[96,896]{1,0:T(8,128)(2,1)S(1)} %get-tuple-element.158), channel_id=1, source_target_pairs={{0,2},{1,3},{2,0},{3,1},{4,6},{5,7},{6,4},{7,5},{8,10},{9,11},{10,... | collective-permute-start | bytes 516104 | tf_op jit(solution)/shard_map/cond/branch_1_fun/ppermute | solution.py:31
  494.9 34.7 %collective-permute-start.74 = (bf16[96,896]{1,0:T(8,128)(2,1)S(1)}, bf16[96,896]{1,0:T(8,128)(2,1)S(1)}, u32[]{:S(2)}, u32[]{:S(2)}) collective-permute-start(bf16[96,896]{1,0:T(8,128)(2,1)S(1)} %get-tuple-element.158), channel_id=1, source_target_pairs={{0,3},{1,2},{2,1},{3,0},{4,7},{5,6},{6,5},{7,4},{8,11},{9,10},{10,... | collective-permute-start | bytes 516104 | tf_op jit(solution)/shard_map/cond/branch_1_fun/ppermute | solution.py:31
  529.7 11.0 %collective-permute-start.75 = (bf16[384,896]{1,0:T(8,128)(2,1)S(1)}, bf16[384,896]{1,0:T(8,128)(2,1)S(1)}, u32[]{:S(2)}, u32[]{:S(2)}) collective-permute-start(bf16[384,896]{1,0:T(8,128)(2,1)S(1)} %constant_dynamic-update-slice_fusion.56), channel_id=1, source_target_pairs={{0,4},{4,0},{8,12},{12,8},{1,5},{5,1},{9,13},{13,9},{2,6},{6,2},{1... | collective-permute-start | bytes 2064392 | tf_op jit(solution)/shard_map/cond/branch_1_fun/ppermute | solution.py:31
  531.2 19.5 %collective-permute-start.76 = (bf16[384,896]{1,0:T(8,128)(2,1)S(1)}, bf16[384,896]{1,0:T(8,128)(2,1)S(1)}, u32[]{:S(2)}, u32[]{:S(2)}) collective-permute-start(bf16[384,896]{1,0:T(8,128)(2,1)S(1)} %constant_dynamic-update-slice_fusion.56), channel_id=1, source_target_pairs={{0,8},{4,12},{8,0},{12,4},{1,9},{5,13},{9,1},{13,5},{2,10},{6,14},... | collective-permute-start | bytes 2064392 | tf_op jit(solution)/shard_map/cond/branch_1_fun/ppermute | solution.py:31
  534.3 16.4 %collective-permute-start.77 = (bf16[384,896]{1,0:T(8,128)(2,1)S(1)}, bf16[384,896]{1,0:T(8,128)(2,1)S(1)}, u32[]{:S(2)}, u32[]{:S(2)}) collective-permute-start(bf16[384,896]{1,0:T(8,128)(2,1)S(1)} %constant_dynamic-update-slice_fusion.56), channel_id=1, source_target_pairs={{0,12},{4,8},{8,4},{12,0},{1,13},{5,9},{9,5},{13,1},{2,14},{6,10},... | collective-permute-start | bytes 2064392 | tf_op jit(solution)/shard_map/cond/branch_1_fun/ppermute | solution.py:31
  535.8 22.0 %collective-permute-start.95 = (bf16[384,2048]{1,0:T(8,128)(2,1)S(1)}, bf16[384,2048]{1,0:T(8,128)(2,1)S(1)}, u32[]{:S(2)}, u32[]{:S(2)}) collective-permute-start(bf16[384,2048]{1,0:T(8,128)(2,1)S(1)} %get-tuple-element.235), channel_id=1, source_target_pairs={{0,1},{1,2},{4,5},{5,6},{8,9},{9,10},{12,13},{13,14},{16,17},{17,1... | collective-permute-start | bytes 4718600 | tf_op jit(solution)/shard_map/cond/branch_1_fun/ppermute | solution.py:170
  537.2 20.6 %collective-permute-start.98 = (bf16[384,2048]{1,0:T(8,128)(2,1)S(1)}, bf16[384,2048]{1,0:T(8,128)(2,1)}, u32[]{:S(2)}, u32[]{:S(2)}) collective-permute-start(bf16[384,2048]{1,0:T(8,128)(2,1)S(1)} %get-tuple-element.236), channel_id=1, source_target_pairs={{2,1},{3,2},{6,5},{7,6},{10,9},{11,10},{14,13},{15,14},{18,17},{19... | collective-permute-start | bytes 4718600 | tf_op jit(solution)/shard_map/cond/branch_1_fun/ppermute | solution.py:174
  556.4 46.3 %collective-permute-start.78 = (bf16[1536,1536]{1,0:T(8,128)(2,1)}, bf16[1536,1536]{1,0:T(8,128)(2,1)}, u32[]{:S(2)}, u32[]{:S(2)}) collective-permute-start(bf16[1536,1536]{1,0:T(8,128)(2,1)} %branch_1_fun.7.mine_ref), channel_id=1, source_target_pairs={{0,16},{16,0},{1,17},{17,1},{2,18},{18,2},{3,19},{19,3},{4,20},{20... | collective-permute-start | bytes 14155784 | tf_op jit(solution)/shard_map/cond/branch_1_fun/ppermute | solution.py:31
  560.7 35.9 %collective-permute-start.96 = (bf16[384,2048]{1,0:T(8,128)(2,1)S(1)}, bf16[384,2048]{1,0:T(8,128)(2,1)S(1)}, u32[]{:S(2)}, u32[]{:S(2)}) collective-permute-start(bf16[384,2048]{1,0:T(8,128)(2,1)S(1)} %get-tuple-element.231), channel_id=1, source_target_pairs={{0,1},{1,2},{2,3},{4,5},{5,6},{6,7},{8,9},{9,10},{10,11},{12,13},{... | collective-permute-start | bytes 4718600 | tf_op jit(solution)/shard_map/cond/branch_1_fun/ppermute | solution.py:170
  562.4 38.4 %collective-permute-start.99 = (bf16[384,2048]{1,0:T(8,128)(2,1)S(1)}, bf16[384,2048]{1,0:T(8,128)(2,1)S(1)}, u32[]{:S(2)}, u32[]{:S(2)}) collective-permute-start(bf16[384,2048]{1,0:T(8,128)(2,1)S(1)} %get-tuple-element.232), channel_id=1, source_target_pairs={{1,0},{2,1},{3,2},{5,4},{6,5},{7,6},{9,8},{10,9},{11,10},{13,12},{... | collective-permute-start | bytes 4718600 | tf_op jit(solution)/shard_map/cond/branch_1_fun/ppermute | solution.py:174
  (2 other events, 3.5 us)
Sparse Core Ops, SparseCore 0:
  16.6 132.8 all-gather.12
  151.2 66.0 all-gather.14
  273.0 167.9 all-gather.16
